TPU v7x, 32 devices: a whole 2x2x4 slice. The times are simulated.
32 devices in a mesh: ctx: 4 (over y, x), head: 8 (over z, core).
Axes of the slice: x: 2, y: 2, z: 4, core: 2. Of those that a mesh axis runs over, the one named last changes fastest.
Arguments:
- attn_in: bfloat16 [8192, 8192], P('ctx', 'head'), may hold values from -6 to 6
- w_key: bfloat16 [8192, 1024], P('head'), may hold values from -0.09375 to 0.09375
- w_value: bfloat16 [8192, 1024], P('head'), may hold values from -0.09375 to 0.09375
- ssm_in: bfloat16 [8192, 8192], P('ctx', 'head'), may hold values from -6 to 6
- gate: bfloat16 [8192, 8192], P('ctx', 'head'), may hold values from -6 to 6
- in_b: bfloat16 [8192, 256], P('ctx'), may hold values from -0.0234375 to 0.0234375
- in_c: bfloat16 [8192, 256], P('ctx'), may hold values from -6 to 6
- rate: float32 [128, 8192], P('head', 'ctx'), may hold values from 0 to 1
- skip: float32 [128], P('head'), may hold values from 0.5 to 2
- gain: float32 [8192], P('head'), may hold values from 0.5 to 1.5
- page_table: int32 [32, 8, 2], replicated, may hold values from 0 to 7, as said below
Outputs:
- mixer_out: bfloat16 [8192, 8192], P('ctx', 'head')
- kv_cache: bfloat16 [32, 2, 1024, 256], P('ctx', None, 'head')
- kv_scale: bfloat16 [32, 2, 16], P('ctx', None, 'head')
Inputs may be any that keep to these rules, and one draw needn't show every extreme that they name: page_table[p, k] = (o, r): head k's columns of page p go to context index o (0 to 3), slot r (0 to 7). For each key-value head, one context shard sends at most 2 of its pages to one owner, and some shard exactly 2; every owner receives at most 8 pages and one owner exactly 8; an owner's slots are 0, 1, 2 and so on, in increasing order of the page's index in the prompt.
All inputs are finite; a program needn't handle non-finite values. Where the computation divides by a largest or mean magnitude, that divisor is 1e-20 or more.
Results may differ from a plain program's by a relative error of at most 0.0053.
Values may be sent and summed in bfloat16 or wider, within the bound.
A program may use at most 192 MiB of HBM per device.

v0:
```python
import jax
import jax.numpy as jnp
from jax import lax
from jax.sharding import PartitionSpec as P

NH = 128
P_SIZE = 64
SPAN = 256
HD = 128
PAGE = 256
GROUP = 64


def carried_in(part, axis, combine, identity):
    place = lax.axis_index(axis)
    gathered = jax.tree.map(lambda a: lax.all_gather(a, axis), part)
    state = jax.tree.map(lambda a, e: jnp.zeros_like(a) + jnp.asarray(e, a.dtype), part, identity)

    def one(step, state):
        return combine(
            state, jax.tree.map(lambda a: lax.dynamic_index_in_dim(a, step, 0, False), gathered)
        )

    return lax.fori_loop(0, place, one, state)


def page_ranks(owner_rows):
    count = owner_rows.shape[-1]
    same = owner_rows[..., :, None] == owner_rows[..., None, :]
    earlier = jnp.arange(count)[None, :] < jnp.arange(count)[:, None]
    return jnp.sum(jnp.logical_and(same, earlier).astype(jnp.int32), axis=-1)


def body(attn_in, w_key, w_value, ssm_in, gate, in_b, in_c, rate, skip, gain, page_table):
    tok_rows = ssm_in.shape[0]
    heads_local = rate.shape[0]
    state_dim = in_b.shape[1]
    head_count = lax.axis_size("head")
    ctx_count = lax.axis_size("ctx")
    spans = tok_rows // SPAN
    cumulative = jnp.cumsum((-rate).reshape(heads_local, spans, SPAN), axis=2)
    b_blocks = in_b.reshape(spans, SPAN, state_dim)
    c_blocks = in_c.reshape(spans, SPAN, state_dim)
    x_blocks = ssm_in.reshape(spans, SPAN, heads_local, P_SIZE)
    cross = jnp.einsum("cqn,ckn->cqk", c_blocks, b_blocks, preferred_element_type=jnp.float32)
    causal = jnp.arange(SPAN)[:, None] >= jnp.arange(SPAN)[None, :]
    spread = cumulative[:, :, :, None] - cumulative[:, :, None, :]
    mixing = (cross[None] * jnp.exp(jnp.where(causal[None, None], spread, -1e30))).astype(
        jnp.bfloat16
    )
    diag_part = jnp.einsum("hcqk,ckhp->cqhp", mixing, x_blocks, preferred_element_type=jnp.float32)
    span_total = cumulative[:, :, -1]
    weights_in = jnp.exp(span_total[:, :, None] - cumulative).transpose(1, 2, 0)
    decayed = (x_blocks * weights_in[..., None]).astype(jnp.bfloat16)
    span_state = jnp.einsum("ckn,ckhp->chnp", b_blocks, decayed, preferred_element_type=jnp.float32)

    def advance(running, span_parts):
        span_log, span_sum = span_parts
        return (jnp.exp(span_log)[:, None, None] * running + span_sum, running)

    empty_state = jnp.zeros((heads_local, state_dim, P_SIZE), jnp.float32)
    device_state, entering_local = lax.scan(advance, empty_state, (span_total.T, span_state))
    device_log = jnp.sum(span_total, axis=1)

    def combine(earlier, latter):
        return (earlier[0] + latter[0], jnp.exp(latter[0])[:, None, None] * earlier[1] + latter[1])

    carried_log, carried_state = carried_in(
        (device_log, device_state),
        "ctx",
        combine,
        (jnp.zeros_like(device_log), jnp.zeros_like(device_state)),
    )
    before_span = jnp.cumsum(span_total, axis=1) - span_total
    entering = entering_local + jnp.exp(before_span).T[:, :, None, None] * carried_state[None]
    entering_b = entering.astype(jnp.bfloat16)
    carried_part = jnp.einsum(
        "cqn,chnp->cqhp", c_blocks, entering_b, preferred_element_type=jnp.float32
    )
    carried_part = carried_part * jnp.exp(cumulative).transpose(1, 2, 0)[..., None]
    output_sum = diag_part + carried_part + skip[None, None, :, None] * x_blocks
    output_sum = output_sum.reshape(tok_rows, heads_local * P_SIZE)
    gated_out = output_sum * jax.nn.silu(gate.astype(jnp.float32))
    square_sum = lax.psum(jnp.sum(gated_out * gated_out, axis=1), "head")
    mean_square = square_sum / (NH * P_SIZE)
    mixer_out = (gated_out * lax.rsqrt(mean_square + 1e-05)[:, None] * gain[None, :]).astype(
        jnp.bfloat16
    )
    kv_width = w_key.shape[1] // head_count
    feature_rows = w_key.shape[0]
    w_both = jnp.stack(
        (
            w_key.reshape(feature_rows, head_count, kv_width),
            w_value.reshape(feature_rows, head_count, kv_width),
        ),
        axis=2,
    )
    w_both = w_both.reshape(feature_rows, head_count * 2 * kv_width)
    kv_rows = lax.psum_scatter(
        lax.dot_general(
            w_both, attn_in, (((0,), (1,)), ((), ())), preferred_element_type=jnp.float32
        ),
        "head",
        scatter_dimension=0,
        tiled=True,
    )
    pages_dev = tok_rows // PAGE
    groups = kv_width // GROUP
    by_page = kv_rows.reshape(2, kv_width, pages_dev, PAGE).transpose(2, 0, 1, 3)
    grouped = by_page.reshape(pages_dev, 2, groups, GROUP, PAGE)
    page_max = jnp.max(jnp.abs(grouped), axis=(3, 4))
    quantized = (grouped / (page_max[..., None, None] + 1e-06)).astype(jnp.bfloat16)
    quantized = quantized.reshape(pages_dev, 2, kv_width, PAGE)
    scale_part = page_max.astype(jnp.bfloat16)
    cap_pages = (pages_dev + ctx_count - 1) // ctx_count
    slot_count = min(ctx_count * cap_pages, 2 * pages_dev)
    ctx_index = lax.axis_index("ctx")
    kv_head = lax.axis_index("head") * kv_width // HD
    head_table = lax.dynamic_index_in_dim(page_table, kv_head, 1, keepdims=False)
    owners_all = head_table[:, 0].reshape(ctx_count, pages_dev)
    slots_all = head_table[:, 1].reshape(ctx_count, pages_dev)
    ranks_all = page_ranks(owners_all)
    own_owners = lax.dynamic_index_in_dim(owners_all, ctx_index, 0, keepdims=False)
    own_ranks = lax.dynamic_index_in_dim(ranks_all, ctx_index, 0, keepdims=False)
    owner_hit = jnp.arange(ctx_count)[:, None, None] == own_owners[None, None, :]
    rank_hit = jnp.arange(cap_pages)[None, :, None] == own_ranks[None, None, :]
    send_mask = jnp.logical_and(owner_hit, rank_hit).astype(jnp.bfloat16)
    send_pages = jnp.einsum(
        "oci,iskt->ocskt", send_mask, quantized, preferred_element_type=jnp.float32
    ).astype(jnp.bfloat16)
    send_scales = jnp.einsum(
        "oci,isg->ocsg", send_mask, scale_part, preferred_element_type=jnp.float32
    ).astype(jnp.bfloat16)
    got_pages, got_scales = (
        lax.all_to_all(send_pages, "ctx", split_axis=0, concat_axis=0, tiled=True),
        lax.all_to_all(send_scales, "ctx", split_axis=0, concat_axis=0, tiled=True),
    )
    to_owner = (owners_all == ctx_index)[None, :, None, :]
    rank_match = (ranks_all[:, None, :] == jnp.arange(cap_pages)[None, :, None])[None]
    slot_match = slots_all[None, :, None, :] == jnp.arange(slot_count)[:, None, None, None]
    placement = jnp.sum(
        jnp.logical_and(jnp.logical_and(to_owner, rank_match), slot_match).astype(jnp.float32),
        axis=3,
    ).astype(jnp.bfloat16)
    kv_cache = jnp.einsum(
        "lsc,scakt->lakt", placement, got_pages, preferred_element_type=jnp.float32
    ).astype(jnp.bfloat16)
    kv_scale = jnp.einsum(
        "lsc,scag->lag", placement, got_scales, preferred_element_type=jnp.float32
    ).astype(jnp.bfloat16)
    return (mixer_out, kv_cache, kv_scale)


def solution(mesh):
    in_specs = (
        P("ctx", "head"),
        P("head", None),
        P("head", None),
        P("ctx", "head"),
        P("ctx", "head"),
        P("ctx", None),
        P("ctx", None),
        P("head", "ctx"),
        P("head"),
        P("head"),
        P(),
    )
    out_specs = (P("ctx", "head"), P("ctx", None, "head", None), P("ctx", None, "head"))
    return jax.shard_map(body, mesh=mesh, in_specs=in_specs, out_specs=out_specs, check_vma=False)
```

profile of v0, /device:TPU:0, one launch (start us, length us, event | category | flops | bytes accessed | tf_op | source)
XLA Modules:
  0.0 358.5 jit_solution(9902821899389319763)
XLA Ops:
  8.1 1.0 neg.7
  9.2 9.0 %reduce-window.6 = f32[16,8,2,128]{3,1,2,0:T(8,128)S(1)} reduce-window(f32[16,8,2,128]{3,1,2,0:T(8,128)S(1)} %copy.68, f32[]{:T(128)} %constant.72.clone.1), window={size=1x1x1x128 pad=0_0x0_0x0_0x127_0}, to_apply=%region_0.0 | reduce-window | flops 4161536 | bytes 262148 | tf_op jit(solution)/shard_map/reduce-window
  19.5 11.6 %reshape.209 = bf16[8,256,16,64]{3,2,1,0:T(8,128)(2,1)} reshape(bf16[2048,1024]{1,0:T(8,128)(2,1)} %param.18) | data formatting | bytes 8388608 | tf_op jit(solution)/shard_map/reshape | solution.py:44
  31.1 10.3 %copy.74 = bf16[8,256,16,64]{1,3,2,0:T(8,128)(2,1)} copy(bf16[8,256,16,64]{3,2,1,0:T(8,128)(2,1)} %reshape.209) | data formatting | bytes 8388608 | tf_op jit(solution)/shard_map/reshape | solution.py:44
  41.4 6.7 %fusion.21 = f32[8,16,256,64]{2,3,1,0:T(8,128)} fusion(bf16[8,256,256,1]{2,1,3,0:T(8,128)(2,1)S(1)} %bitcast.157, bf16[8,256,16,64]{1,3,2,0:T(8,128)(2,1)} %copy.74, f32[8,256,16]{1,2,0:T(8,128)S(1)} %copy.78), kind=kOutput, calls=%fused_computation.37 | convolution fusion | flops 1080033280 | bytes 13762560 | tf_op jit(solution)/shard_map/ckn,ckhp->chnp/dot_general | solution.py:55
  48.1 73.0 %while.26 = (s32[]{:T(128)}, f32[16,256,64]{2,1,0:T(8,128)S(1)}, f32[8,16,256,64]{3,2,1,0:T(8,128)}, f32[8,16]{1,0:T(8,128)S(1)}, f32[8,16,256,64]{2,3,1,0:T(8,128)}, /*index=5*/s32[]{:T(128)}, s32[]{:T(128)}) while((s32[]{:T(128)}, f32[16,256,64]{2,1,0:T(8,128)S(1)}, f32[8,16,256,64]{3,2,1,0:T(8,128)}, f32[8,16]{1,0:T(8,128)S(1)}, ...), condition=%wide.region_3.4_spmd.clone, body=%wide.region_2.3_spmd.clone.sunk | while | flops 1048579 | bytes 10486560 | solution.py:62
  48.1 1.5 bitcast_dynamic-update-slice_fusion.2
  49.6 2.3 constant_dynamic-slice_fusion.8
  51.9 3.2 copy.122
  55.1 2.1 bitcast_add_fusion.5
  57.2 1.5 bitcast_dynamic-update-slice_fusion.2
  58.7 2.3 constant_dynamic-slice_fusion.8
  61.0 3.2 copy.122
  64.2 2.1 bitcast_add_fusion.5
  66.3 1.5 bitcast_dynamic-update-slice_fusion.2
  67.8 2.3 constant_dynamic-slice_fusion.8
  70.1 3.2 copy.122
  73.3 2.1 bitcast_add_fusion.5
  75.4 1.5 bitcast_dynamic-update-slice_fusion.2
  76.9 2.3 constant_dynamic-slice_fusion.8
  79.2 3.2 copy.122
  82.4 2.1 bitcast_add_fusion.5
  84.6 1.5 bitcast_dynamic-update-slice_fusion.2
  86.1 2.3 constant_dynamic-slice_fusion.8
  88.4 3.2 copy.122
  91.6 2.1 bitcast_add_fusion.5
  93.7 1.4 bitcast_dynamic-update-slice_fusion.2
  95.2 2.3 constant_dynamic-slice_fusion.8
  97.5 3.2 copy.122
  100.7 2.1 bitcast_add_fusion.5
  102.8 1.5 bitcast_dynamic-update-slice_fusion.2
  104.3 2.3 constant_dynamic-slice_fusion.8
  106.6 3.2 copy.122
  109.9 2.1 bitcast_add_fusion.5
  112.0 1.5 bitcast_dynamic-update-slice_fusion.2
  113.5 2.3 constant_dynamic-slice_fusion.8
  115.8 3.2 copy.122
  119.0 2.1 bitcast_add_fusion.5
  121.1 1.6 copy.80
  122.7 2.9 copy.86
  125.6 3.9 %copy.87 = bf16[1024,1024]{0,1:T(8,128)(2,1)} copy(bf16[1024,1024]{1,0:T(8,128)(2,1)} %param.17) | data formatting | bytes 4194304 | tf_op args[2]
  129.5 2.1 pad_maximum_fusion
  132.5 11.7 %fusion.45 = f32[2048,2048]{1,0:T(8,128)} fusion(bf16[1024,2048]{0,1:T(8,128)(2,1)S(1)} %bitcast.169, bf16[2048,1024]{1,0:T(8,128)(2,1)S(1)} %copy-done.8), kind=kOutput, calls=%fused_computation.88 | convolution fusion | flops 8589934592 | bytes 25165824 | tf_op jit(solution)/shard_map/dot_general | solution.py:100
  146.5 12.0 %all-reduce = f32[64]{0:T(128)S(1)} all-reduce(f32[64]{0:T(128)S(1)} %dynamic-update-slice), channel_id=2, replica_groups=mesh['ctx'=4,'head'=8] {'ctx'}, use_global_device_ids=true, to_apply=%add | all-reduce | flops 64 | bytes 512
  158.6 6.6 %copy.85 = bf16[2048,1024]{0,1:T(8,128)(2,1)} copy(bf16[2048,1024]{1,0:T(8,128)(2,1)} %param.19) | data formatting | bytes 8388608 | tf_op args[4]
  166.6 1.8 fusion.44
  168.3 10.0 %all-gather.4.cloned.1.call-done = f32[64,256,64]{1,2,0:T(8,128)} async-done(((f32[16,256,64]{1,2,0:T(8,128)}), f32[64,256,64]{1,2,0:T(8,128)}) %all-gather.4.cloned.1.call-update) | async-done | bytes 4194320 | tf_op jit(solution)/shard_map/all_gather | solution.py:16
  178.4 1.6 broadcast.94
  179.9 9.0 %fusion.14 = f32[8,16,64,256]{3,2,1,0:T(8,128)S(1)} fusion(bf16[8,256,256,1]{2,1,3,0:T(8,128)(2,1)} %bitcast.166, f32[8,16,256,64]{3,2,1,0:T(8,128)} %get-tuple-element.75, f32[16,256,64]{2,1,0:T(8,128)} %get-tuple-element.77, f32[8,16]{1,0:T(8,128)S(1)} %exponential_bitcast_fusion.3), kind=kOutput, calls=%fused_computation.27 | convolution fusion | flops 1080033280 | bytes 18874880 | tf_op jit(solution)/shard_map/cqn,chnp->cqhp/dot_general | solution.py:77
  189.0 10.5 %fusion.9 = f32[8,256,16,64]{1,3,2,0:T(8,128)} fusion(bf16[8,256,16,64]{1,3,2,0:T(8,128)(2,1)S(1)} %copy-done.4, f32[8,16,64,256]{3,2,1,0:T(8,128)S(1)} %fusion.14, f32[16]{0:T(128)S(1)} %copy-done.9, f32[8,256,16]{1,2,0:T(8,128)S(1)} %copy.83, f32[16,8,256]{2,0,1:T(8,128)S(1)} %copy.71, f32[8,256,256]{2,1,0:T(8,128)S(1)} %copy-done.6, ...), kind=kOutput, calls=%fused_computation.22 | convolution fusion | flops 1117782016 | bytes 23396416 | tf_op jit(solution)/shard_map/hcqk,ckhp->cqhp/dot_general | solution.py:51
  199.5 10.0 %copy.84 = f32[8,256,16,64]{1,0,3,2:T(8,128)S(1)} copy(f32[8,256,16,64]{1,3,2,0:T(8,128)} %fusion.9) | data formatting | bytes 16777216 | tf_op jit(solution)/shard_map/add | solution.py:81
  209.5 4.2 %copy.117 = f32[128,8,8,256]{3,1,2,0:T(8,128)S(1)} copy(f32[128,8,8,256]{3,2,1,0:T(8,128)S(1)} %bitcast.161) | data formatting | bytes 16777216
  213.7 3.2 copy-done.2
  216.9 2.7 multiply_reduce_fusion
  219.6 17.8 %psum.7 = f32[2048]{0:T(1024)S(1)} all-reduce(f32[2048]{0:T(1024)S(1)} %multiply_reduce_fusion), channel_id=1, replica_groups=mesh['ctx'=4,'head'=8] {'head'}, use_global_device_ids=true, to_apply=%region_9.10 | all-reduce | flops 2048 | bytes 16384 | tf_op jit(solution)/shard_map/psum | solution.py:84
  237.4 78.9 %reduce-scatter.2.cloned.1.call-done = f32[256,2048]{1,0:T(8,128)} async-done(((f32[2048,2048]{1,0:T(8,128)}), f32[256,2048]{1,0:T(8,128)}) %reduce-scatter.2.cloned.1.call-update) | async-done | bytes 2097168 | tf_op jit(solution)/shard_map/reduce_scatter | solution.py:99
  316.3 2.5 copy.118
  319.9 1.8 copy.88
  321.8 8.1 %all_to_all.10 = bf16[4,2,2,2]{3,1,2,0:T(2,128)(2,1)S(1)} all-to-all(bf16[4,2,2,2]{3,1,2,0:T(2,128)(2,1)S(1)} %copy.91), channel_id=1, replica_groups=mesh['ctx'=4,'head'=8] {'ctx'}, dimensions={0} | all-to-all | bytes 128 | tf_op jit(solution)/shard_map/all_to_all | solution.py:136
  329.9 3.5 all-to-all-start
  333.4 7.8 %multiply_convert_fusion.2 = bf16[2048,1024]{0,1:T(8,128)(2,1)} fusion(f32[1024]{0:T(1024)S(1)} %copy-done.7, f32[2048]{0:T(1024)S(1)} %add_rsqrt_fusion, f32[2048,1024]{0,1:T(8,128)} %bitcast.160, bf16[2048,1024]{0,1:T(8,128)(2,1)} %copy.85), kind=kLoop, calls=%fused_computation.30 | loop fusion | flops 18874368 | bytes 16789504 | tf_op jit(solution)/shard_map/convert_element_type | solution.py:86
  341.2 6.4 %copy.94 = bf16[2048,1024]{1,0:T(8,128)(2,1)} copy(bf16[2048,1024]{0,1:T(8,128)(2,1)} %multiply_convert_fusion.2) | data formatting | bytes 8388608
  348.4 1.5 bitcast_convert_fusion
  349.9 1.2 copy.95
  (81 shorter events, 7.3 us)
Async XLA Ops:
  8.0 33.4 %copy-start = (bf16[2048,256]{1,0:T(8,128)(2,1)S(1)}, bf16[2048,256]{1,0:T(8,128)(2,1)}, u32[]{:S(2)}) copy-start(bf16[2048,256]{1,0:T(8,128)(2,1)} %param.20) | copy-start | bytes 3145732
  8.0 170.3 %all-gather.4.cloned.1.call-start = ((), (), s32[]{:S(2)}) async-start(), calls=%async_computation.4 | async-start | bytes 5242880 | tf_op jit(solution)/shard_map/all_gather | solution.py:16
  122.7 193.6 %reduce-scatter.2.cloned.1.call-start = ((), (), s32[]{:S(2)}) async-start(), calls=%async_computation.3 | async-start | bytes 18874368 | tf_op jit(solution)/shard_map/reduce_scatter | solution.py:99
  129.5 3.0 copy-start.8
  144.2 0.7 copy-start.10
  158.6 8.0 %copy-start.5 = (bf16[2048,256]{1,0:T(8,128)(2,1)S(1)}, bf16[2048,256]{1,0:T(8,128)(2,1)}, u32[]{:S(2)}) copy-start(bf16[2048,256]{1,0:T(8,128)(2,1)} %param.21) | copy-start | bytes 3145732
  179.9 9.0 %copy-start.4 = (bf16[8,256,16,64]{1,3,2,0:T(8,128)(2,1)S(1)}, bf16[8,256,16,64]{1,3,2,0:T(8,128)(2,1)}, u32[]{:S(2)}) copy-start(bf16[8,256,16,64]{1,3,2,0:T(8,128)(2,1)} %copy.74) | copy-start | bytes 12582916
  179.9 9.0 %copy-start.6 = (f32[8,256,256]{2,1,0:T(8,128)S(1)}, f32[8,256,256]{2,1,0:T(8,128)}, u32[]{:S(2)}) copy-start(f32[8,256,256]{2,1,0:T(8,128)} %fusion.44) | copy-start | bytes 6291460
  179.9 9.0 %copy-start.9 = (f32[16]{0:T(128)S(1)}, f32[16]{0:T(128)}, u32[]{:S(2)}) copy-start(f32[16]{0:T(128)} %param.23) | copy-start | bytes 196
  209.5 7.4 %copy-start.3 = (bf16[2048,1024]{0,1:T(8,128)(2,1)S(1)}, bf16[2048,1024]{0,1:T(8,128)(2,1)}, u32[]{:S(2)}) copy-start(bf16[2048,1024]{0,1:T(8,128)(2,1)} %copy.85) | copy-start | bytes 12582916
  213.7 3.2 copy-start.2
  319.3 14.1 %copy-start.7 = (f32[1024]{0:T(1024)S(1)}, f32[1024]{0:T(1024)}, u32[]{:S(2)}) copy-start(f32[1024]{0:T(1024)} %param.24) | copy-start | bytes 12292
  329.9 18.5 %all-to-all-start = ((bf16[4,2,2,128,256]{4,1,3,2,0:T(2,128)(2,1)}), bf16[4,2,2,128,256]{4,1,3,2,0:T(2,128)(2,1)S(1)}, u32[]{:S(2)}, u32[]{:S(2)}) async-start(bf16[4,2,2,128,256]{4,1,3,2,0:T(2,128)(2,1)} %copy.88), calls=%async_computation.1 | async-start | bytes 2097152 | tf_op jit(solution)/shard_map/all_to_all | solution.py:135
  347.6 3.5 copy-start.1
Sparse Core Ops, SparseCore 0:
  122.8 55.5 all-gather.3
Sparse Core Ops, SparseCore 1:
  144.4 171.9 reduce-scatter.1
where the time goes:
time: 361 us; the launch traced here: 359 us
  local copies, waits for them, and re-layouts  116 us (32%)
  waiting for transfers between devices  89 us (25%)
  other arithmetic  52.6 us (15%)
  matrix products  42.6 us (12%)
  blocking collectives  37.8 us (10%)
  between operations  16.5 us (5%)
    reduce_scatter x1, waiting for transfers between devices, body(): lax.psum_scatter(lax.dot_general(w_both, attn_in, (((0,), (1,)), ((), ())...  78.9 us
    dynamic_slice x16, local copies, waits for them, and re-layouts, body(): lax.scan(advance, empty_state, (span_total.T, span_state))  44.1 us
    unnamed x32, local copies, waits for them, and re-layouts  33.2 us
    reshape x2, local copies, waits for them, and re-layouts, body(): x_blocks = ssm_in.reshape(spans, SPAN, heads_local, P_SIZE)  21.9 us
    psum x1, blocking collectives, body(): square_sum = lax.psum(jnp.sum(gated_out * gated_out, axis=1), 'head')  17.8 us
    add x8, other arithmetic, advance(): return (jnp.exp(span_log)[:, None, None] * running + span_sum, running)  16.7 us
    unnamed x1, blocking collectives  12 us
    dynamic_update_slice x8, other arithmetic, body(): lax.scan(advance, empty_state, (span_total.T, span_state))  11.9 us
  transfers between devices with their start and end apart: 3, of which 2 were waited for; matrix products, arithmetic and copies ran while one was open for 24% of the time, Pallas kernels for 0%

commit v1 on v0

v1 whole, which is shorter than its diff:
```python
import jax
import jax.numpy as jnp
from jax import lax
from jax.sharding import PartitionSpec as P
from jax.experimental import pallas as pl
from jax.experimental.pallas import tpu as pltpu

NH = 128
P_SIZE = 64
SPAN = 256
HD = 128
PAGE = 256
GROUP = 64


LOG2E = 1.4426950408889634
F32 = jnp.float32


def lanes_of_pair(columns, p, lane_low):
    rows = columns.shape[0]
    first = jnp.broadcast_to(columns[:, 2 * p : 2 * p + 1], (rows, 2 * P_SIZE))
    second = jnp.broadcast_to(columns[:, 2 * p + 1 : 2 * p + 2], (rows, 2 * P_SIZE))
    return jnp.where(lane_low, first, second)


def state_kernel(x_ref, b_ref, col_ref, decay_ref, ent_ref, last_ref, run):
    k = pl.program_id(0)

    @pl.when(k == 0)
    def _():
        run[...] = jnp.zeros_like(run)

    ent_ref[0] = run[...]
    cum = col_ref[...]
    weights = jnp.exp2(cum[SPAN - 1 :, :] - cum)
    lane_low = lax.broadcasted_iota(jnp.int32, (SPAN, 2 * P_SIZE), 1) < P_SIZE
    b_t = b_ref[...].T
    for p in range(cum.shape[1] // 2):
        at = slice(p * 2 * P_SIZE, (p + 1) * 2 * P_SIZE)
        decayed = (x_ref[:, at].astype(F32) * lanes_of_pair(weights, p, lane_low)).astype(jnp.bfloat16)
        part = jnp.dot(b_t, decayed, preferred_element_type=F32)
        run[:, at] = run[:, at] * decay_ref[0, :, at] + part

    @pl.when(k == pl.num_programs(0) - 1)
    def _():
        last_ref[...] = run[...]


def mix_kernel(x_ref, g_ref, b_ref, c_ref, col_ref, row_ref, ent_ref, car_ref, bef_ref, skip_ref, o_ref, s_ref):
    c = c_ref[...]
    cross = lax.dot_general(c, b_ref[...], (((1,), (1,)), ((), ())), preferred_element_type=F32)
    t_at = lax.broadcasted_iota(jnp.int32, (SPAN, SPAN), 0)
    u_at = lax.broadcasted_iota(jnp.int32, (SPAN, SPAN), 1)
    cross = jnp.where(u_at <= t_at, cross, 0.0)
    cum = col_ref[...]
    leaving = jnp.exp2(cum)
    lane_low = lax.broadcasted_iota(jnp.int32, (SPAN, 2 * P_SIZE), 1) < P_SIZE
    total = jnp.zeros((SPAN, 2 * P_SIZE), F32)
    for p in range(cum.shape[1] // 2):
        at = slice(p * 2 * P_SIZE, (p + 1) * 2 * P_SIZE)
        x = x_ref[:, at].astype(F32)
        out = skip_ref[:, at] * x
        entering = (ent_ref[0, :, at] + bef_ref[0, :, at] * car_ref[:, at]).astype(jnp.bfloat16)
        out += lanes_of_pair(leaving, p, lane_low) * jnp.dot(c, entering, preferred_element_type=F32)
        for i in range(2):
            h = 2 * p + i
            spread = jnp.minimum(cum[:, h : h + 1] - row_ref[h : h + 1, :], 0.0)
            mixing = (cross * jnp.exp2(spread)).astype(jnp.bfloat16)
            mine = jnp.where(lane_low == (i == 0), x, 0.0).astype(jnp.bfloat16)
            out += jnp.dot(mixing, mine, preferred_element_type=F32)
        gate = g_ref[:, at].astype(F32)
        out = out * (gate / (1.0 + jnp.exp2(gate * -LOG2E)))
        o_ref[:, at] = out
        total += out * out
    s_ref[...] = jnp.sum(total, axis=1, keepdims=True)


def page_ranks(owner_rows):
    count = owner_rows.shape[-1]
    same = owner_rows[..., :, None] == owner_rows[..., None, :]
    earlier = jnp.arange(count)[None, :] < jnp.arange(count)[:, None]
    return jnp.sum(jnp.logical_and(same, earlier).astype(jnp.int32), axis=-1)


def body(attn_in, w_key, w_value, ssm_in, gate, in_b, in_c, rate, skip, gain, page_table):
    tok_rows, width = ssm_in.shape
    heads_local = rate.shape[0]
    state_dim = in_b.shape[1]
    head_count = lax.axis_size("head")
    ctx_count = lax.axis_size("ctx")
    spans = tok_rows // SPAN
    kv_width = w_key.shape[1] // head_count
    feature_rows = w_key.shape[0]
    w_both = jnp.stack(
        (
            w_key.reshape(feature_rows, head_count, kv_width),
            w_value.reshape(feature_rows, head_count, kv_width),
        ),
        axis=2,
    )
    w_both = w_both.reshape(feature_rows, head_count * 2 * kv_width)
    kv_part = lax.dot_general(
        w_both, attn_in, (((0,), (1,)), ((), ())), preferred_element_type=jnp.float32
    )
    kv_rows = lax.psum_scatter(kv_part, "head", scatter_dimension=0, tiled=True)

    upto = (jnp.arange(SPAN)[:, None] <= jnp.arange(SPAN)[None, :]).astype(F32)
    cum = jnp.einsum(
        "hcu,ut->hct", rate.reshape(heads_local, spans, SPAN) * -LOG2E, upto,
        precision=lax.Precision.HIGHEST,
    )
    span_total = cum[:, :, -1]
    cum_row = cum.reshape(heads_local, tok_rows)
    cum_col = cum_row.T
    before_span = jnp.cumsum(span_total, axis=1) - span_total

    def per_lane(values):
        return jnp.repeat(values, P_SIZE, axis=0).T.reshape(-1, 1, width)

    decay = per_lane(jnp.exp2(span_total))
    before = per_lane(jnp.exp2(before_span))
    rows = lambda w: pl.BlockSpec((SPAN, w), lambda k: (k, 0))
    lane_rows = pl.BlockSpec((1, 1, width), lambda k: (k, 0, 0))
    states = pl.BlockSpec((1, state_dim, width), lambda k: (k, 0, 0))
    whole = lambda *s: pl.BlockSpec(s, lambda k: (0,) * len(s))
    params = pltpu.CompilerParams(vmem_limit_bytes=48 * 1024 * 1024)
    entering, device_state = pl.pallas_call(
        state_kernel,
        grid=(spans,),
        in_specs=[rows(width), rows(state_dim), rows(heads_local), lane_rows],
        out_specs=[states, whole(state_dim, width)],
        out_shape=[
            jax.ShapeDtypeStruct((spans, state_dim, width), F32),
            jax.ShapeDtypeStruct((state_dim, width), F32),
        ],
        scratch_shapes=[pltpu.VMEM((state_dim, width), F32)],
        compiler_params=params,
        cost_estimate=pl.CostEstimate(flops=10**10, bytes_accessed=20 * 2**20, transcendentals=0),
    )(ssm_in, in_b, cum_col, decay)
    device_total = jnp.sum(span_total, axis=1)
    all_states = lax.all_gather(device_state, "ctx")
    all_totals = lax.all_gather(device_total, "ctx")
    place = lax.axis_index("ctx")
    earlier = jnp.arange(ctx_count) < place
    between = jnp.sum(
        jnp.where(
            ((jnp.arange(ctx_count)[None, :] > jnp.arange(ctx_count)[:, None]) & earlier[None, :])[:, :, None],
            all_totals[None],
            0.0,
        ),
        axis=1,
    )
    weight = jnp.where(earlier[:, None], jnp.exp2(between), 0.0)
    carried = jnp.sum(all_states * jnp.repeat(weight, P_SIZE, axis=1)[:, None, :], axis=0)
    gated_out, square_sum = pl.pallas_call(
        mix_kernel,
        grid=(spans,),
        in_specs=[
            rows(width), rows(width), rows(state_dim), rows(state_dim), rows(heads_local),
            pl.BlockSpec((heads_local, SPAN), lambda k: (0, k)),
            states, whole(state_dim, width), lane_rows, whole(1, width),
        ],
        out_specs=[rows(width), rows(1)],
        out_shape=[
            jax.ShapeDtypeStruct((tok_rows, width), F32),
            jax.ShapeDtypeStruct((tok_rows, 1), F32),
        ],
        compiler_params=params,
        cost_estimate=pl.CostEstimate(flops=3 * 10**10, bytes_accessed=40 * 2**20, transcendentals=0),
    )(ssm_in, gate, in_b, in_c, cum_col, cum_row, entering, carried, before,
      jnp.repeat(skip, P_SIZE).reshape(1, width))
    mean_square = lax.psum(square_sum[:, 0], "head") / (NH * P_SIZE)
    mixer_out = (gated_out * lax.rsqrt(mean_square + 1e-05)[:, None] * gain[None, :]).astype(
        jnp.bfloat16
    )
    pages_dev = tok_rows // PAGE
    groups = kv_width // GROUP
    by_page = kv_rows.reshape(2, kv_width, pages_dev, PAGE).transpose(2, 0, 1, 3)
    grouped = by_page.reshape(pages_dev, 2, groups, GROUP, PAGE)
    page_max = jnp.max(jnp.abs(grouped), axis=(3, 4))
    quantized = (grouped / (page_max[..., None, None] + 1e-06)).astype(jnp.bfloat16)
    quantized = quantized.reshape(pages_dev, 2, kv_width, PAGE)
    scale_part = page_max.astype(jnp.bfloat16)
    cap_pages = (pages_dev + ctx_count - 1) // ctx_count
    slot_count = min(ctx_count * cap_pages, 2 * pages_dev)
    ctx_index = lax.axis_index("ctx")
    kv_head = lax.axis_index("head") * kv_width // HD
    head_table = lax.dynamic_index_in_dim(page_table, kv_head, 1, keepdims=False)
    owners_all = head_table[:, 0].reshape(ctx_count, pages_dev)
    slots_all = head_table[:, 1].reshape(ctx_count, pages_dev)
    ranks_all = page_ranks(owners_all)
    own_owners = lax.dynamic_index_in_dim(owners_all, ctx_index, 0, keepdims=False)
    own_ranks = lax.dynamic_index_in_dim(ranks_all, ctx_index, 0, keepdims=False)
    owner_hit = jnp.arange(ctx_count)[:, None, None] == own_owners[None, None, :]
    rank_hit = jnp.arange(cap_pages)[None, :, None] == own_ranks[None, None, :]
    send_mask = jnp.logical_and(owner_hit, rank_hit).astype(jnp.bfloat16)
    send_pages = jnp.einsum(
        "oci,iskt->ocskt", send_mask, quantized, preferred_element_type=jnp.float32
    ).astype(jnp.bfloat16)
    send_scales = jnp.einsum(
        "oci,isg->ocsg", send_mask, scale_part, preferred_element_type=jnp.float32
    ).astype(jnp.bfloat16)
    got_pages, got_scales = (
        lax.all_to_all(send_pages, "ctx", split_axis=0, concat_axis=0, tiled=True),
        lax.all_to_all(send_scales, "ctx", split_axis=0, concat_axis=0, tiled=True),
    )
    to_owner = (owners_all == ctx_index)[None, :, None, :]
    rank_match = (ranks_all[:, None, :] == jnp.arange(cap_pages)[None, :, None])[None]
    slot_match = slots_all[None, :, None, :] == jnp.arange(slot_count)[:, None, None, None]
    placement = jnp.sum(
        jnp.logical_and(jnp.logical_and(to_owner, rank_match), slot_match).astype(jnp.float32),
        axis=3,
    ).astype(jnp.bfloat16)
    kv_cache = jnp.einsum(
        "lsc,scakt->lakt", placement, got_pages, preferred_element_type=jnp.float32
    ).astype(jnp.bfloat16)
    kv_scale = jnp.einsum(
        "lsc,scag->lag", placement, got_scales, preferred_element_type=jnp.float32
    ).astype(jnp.bfloat16)
    return (mixer_out, kv_cache, kv_scale)


def solution(mesh):
    in_specs = (
        P("ctx", "head"),
        P("head", None),
        P("head", None),
        P("ctx", "head"),
        P("ctx", "head"),
        P("ctx", None),
        P("ctx", None),
        P("head", "ctx"),
        P("head"),
        P("head"),
        P(),
    )
    out_specs = (P("ctx", "head"), P("ctx", None, "head", None), P("ctx", None, "head"))
    return jax.shard_map(body, mesh=mesh, in_specs=in_specs, out_specs=out_specs, check_vma=False)
```

time: 361 us -> 256 us (0.71)
  local copies, waits for them, and re-layouts: 116 us -> 18.5 us
  other arithmetic: 52.6 us -> 12.7 us
  waiting for transfers between devices: 89 us -> 120 us
  Pallas kernels: 0 us -> 30.9 us
  matrix products: 42.6 us -> 15 us
    dynamic_slice x16 -> x0, local copies, waits for them, and re-layouts: 44.1 us -> none  [body(): lax.scan(advance, empty_state, (span_total.T, span_state))]
    pallas_call x0 -> x2, Pallas kernels: none -> 30.9 us  [the longest x1 19.3 us: body(): pl.pallas_call(mix_kernel, grid=(spans,), in_specs=[rows(width), rows(wid...]
    dot_general x4 -> x1, matrix products: 28 us -> 0.24 us  [body(): jnp.einsum('hcu,ut->hct', rate.reshape(heads_local, spans, SPAN) * -LOG2E...]
    reshape x4, local copies, waits for them, and re-layouts: 22 us -> 0.24 us  [per_lane(): return jnp.repeat(values, P_SIZE, axis=0).T.reshape(-1, 1, width)]
    unnamed x32 -> x27, local copies, waits for them, and re-layouts: 33.2 us -> 15.1 us
    reduce_scatter x1, waiting for transfers between devices: 78.9 us -> 96 us  [body(): kv_rows = lax.psum_scatter(kv_part, 'head', scatter_dimension=0, tiled=True)]
    add x8 -> x0, other arithmetic: 16.7 us -> none  [advance(): return (jnp.exp(span_log)[:, None, None] * running + span_sum, running)]
    dynamic_update_slice x8 -> x0, other arithmetic: 11.9 us -> none  [body(): lax.scan(advance, empty_state, (span_total.T, span_state))]
  transfers between devices with their start and end apart: 3 -> 3, of which waited for: 2 -> 3; matrix products, arithmetic and copies ran while one was open for 24% -> 13% of each run, Pallas kernels for 0% -> 8%
where the time goes in v1:
time: 256 us; the launch traced here: 255 us
  waiting for transfers between devices  120 us (47%)
  blocking collectives  38.3 us (15%)
  Pallas kernels  30.9 us (12%)
  local copies, waits for them, and re-layouts  18.5 us (7%)
  between operations  16.4 us (6%)
  matrix products  15 us (6%)
  other arithmetic  12.7 us (5%)
  starting transfers between devices  3.6 us (1%)
    reduce_scatter x1, waiting for transfers between devices, body(): kv_rows = lax.psum_scatter(kv_part, 'head', scatter_dimension=0, tiled=True)  96 us
    pallas_call x1, Pallas kernels, body(): pl.pallas_call(mix_kernel, grid=(spans,), in_specs=[rows(width), rows(wid...  19.3 us
    all_gather x1, waiting for transfers between devices, body(): all_states = lax.all_gather(device_state, 'ctx')  18.8 us
    psum x1, blocking collectives, body(): mean_square = lax.psum(square_sum[:, 0], 'head') / (NH * P_SIZE)  18.3 us
    unnamed x27, local copies, waits for them, and re-layouts  15.1 us
    unnamed x1, blocking collectives  11.9 us
    dot_general x1, matrix products, body(): lax.dot_general(w_both, attn_in, (((0,), (1,)), ((), ())), preferred_elem...  11.7 us
    pallas_call x1, Pallas kernels, body(): pl.pallas_call(state_kernel, grid=(spans,), in_specs=[rows(width), rows(s...  11.7 us
  transfers between devices with their start and end apart: 3, of which 3 were waited for; matrix products, arithmetic and copies ran while one was open for 13% of the time, Pallas kernels for 8%

profile of v1, /device:TPU:0, one launch (start us, length us, event | category | flops | bytes accessed | tf_op | source)
XLA Modules:
  0.0 254.9 jit_solution(1569835624214664454)
XLA Ops:
  8.0 0.0 copy-start
  8.0 0.0 all-gather.4.cloned.1.call-start
  8.1 0.9 broadcast_multiply_fusion
  9.0 0.2 fusion.8
  9.3 0.3 slice_reduce_fusion.2
  9.6 0.1 copy.34
  9.7 0.1 broadcast_in_dim.40
  9.8 0.1 reshape.160
  10.0 0.3 copy.36.col_ref
  10.3 0.0 copy-start.2
  10.3 1.2 copy-done.2
  11.6 11.7 %shard_map.130 = (f32[8,256,1024]{2,1,0:T(8,128)}, f32[256,1024]{1,0:T(8,128)}) custom-call(bf16[2048,1024]{1,0:T(8,128)(2,1)} %x_ref.3, bf16[2048,256]{1,0:T(8,128)(2,1)S(1)} %copy-done.2, f32[2048,16]{1,0:T(8,128)S(1)} %copy.36.col_ref, f32[8,1,1024]{2,1,0:T(1,128)S(1)} %reshape.161.decay_ref), custom_call_target="tpu_custom_call" | custom-call | flops 10000000000 | bytes 20971520 | tf_op jit(solution)/shard_map/pallas_call | solution.py:128
  23.2 0.0 all-gather.4.cloned.1.call-update
  23.2 0.0 reduce-scatter.2.cloned.1.call-start
  23.3 2.9 %copy.37 = bf16[1024,1024]{0,1:T(8,128)(2,1)S(1)} copy(bf16[1024,1024]{1,0:T(8,128)(2,1)} %param.12) | data formatting | bytes 4194304 | tf_op args[1]
  26.2 3.9 %copy.38 = bf16[1024,1024]{0,1:T(8,128)(2,1)} copy(bf16[1024,1024]{1,0:T(8,128)(2,1)} %param.13) | data formatting | bytes 4194304 | tf_op args[2]
  30.1 2.1 pad_maximum_fusion
  32.2 0.9 copy-done.7
  33.1 11.7 %fusion.21 = f32[2048,2048]{1,0:T(8,128)} fusion(bf16[1024,2048]{0,1:T(8,128)(2,1)S(1)} %bitcast.116, bf16[2048,1024]{1,0:T(8,128)(2,1)S(1)} %copy-done.7), kind=kOutput, calls=%fused_computation.55 | convolution fusion | flops 8589934592 | bytes 25165824 | tf_op jit(solution)/shard_map/dot_general | solution.py:103
  44.8 0.0 reduce-scatter.2.cloned.1.call-update
  44.8 0.0 copy-start.3
  44.9 0.0 copy-done
  44.9 0.1 reshape_squeeze.3
  45.0 0.1 eq.106
  45.1 0.4 copy-done.8
  45.5 0.6 dynamic-slice
  46.7 0.2 dynamic-update-slice
  47.0 11.9 %all-reduce = f32[64]{0:T(128)S(1)} all-reduce(f32[64]{0:T(128)S(1)} %dynamic-update-slice), channel_id=3, replica_groups=mesh['ctx'=4,'head'=8] {'ctx'}, use_global_device_ids=true, to_apply=%add | all-reduce | flops 64 | bytes 512
  58.9 0.1 reshape.167
  59.0 0.1 select_reduce_fusion
  59.1 0.1 exponential_select_fusion
  59.2 0.1 broadcast_in_dim.46
  59.2 0.1 mul.41
  59.3 0.1 broadcast_in_dim.47
  59.4 0.1 reshape.162
  59.5 0.0 copy-done.6
  59.5 0.1 broadcast_in_dim.48
  59.6 0.1 reshape_reshape.3.skip_ref
  59.7 0.2 convert_reduce_fusion.1
  60.0 0.1 convert_reduce_fusion
  60.1 18.8 %all-gather.4.cloned.1.call-done = f32[1024,1024]{1,0:T(8,128)} async-done(((f32[256,1024]{1,0:T(8,128)}), f32[1024,1024]{1,0:T(8,128)}) %all-gather.4.cloned.1.call-update) | async-done | bytes 4194320 | tf_op jit(solution)/shard_map/all_gather | solution.py:142
  78.9 2.9 %multiply_reduce_fusion.car_ref = f32[256,1024]{1,0:T(8,128)S(1)} fusion(f32[4,256,1024]{2,1,0:T(8,128)} %bitcast.115, f32[4,1024]{1,0:T(4,128)S(1)} %mul.41), kind=kLoop, calls=%fused_computation.2 | loop fusion | flops 1835008 | bytes 5259264 | tf_op jit(solution)/shard_map/reduce_sum | solution.py:155
  81.7 0.0 copy-done.3
  81.7 0.0 copy-start.4
  81.8 1.2 copy-done.4
  83.0 19.3 %shard_map.131 = (f32[2048,1024]{1,0:T(8,128)}, f32[2048,1]{1,0:T(8,128)S(1)}) custom-call(bf16[2048,1024]{1,0:T(8,128)(2,1)} %x_ref.3, bf16[2048,1024]{1,0:T(8,128)(2,1)} %g_ref.1, bf16[2048,256]{1,0:T(8,128)(2,1)S(1)} %copy-done.3, bf16[2048,256]{1,0:T(8,128)(2,1)S(1)} %copy-done.4, f32[2048,16]{1,0:T(8,128)S(1)} %copy.36.col_ref, ...), custom_call_target="tpu_custom_call" | custom-call | flops 30000001024 | bytes 41943040 | tf_op jit(solution)/shard_map/pallas_call | solution.py:156
  102.3 0.3 reduce.3
  102.6 18.3 %psum.7 = f32[2048]{0:T(1024)S(1)} all-reduce(f32[2048]{0:T(1024)S(1)} %reduce.3), channel_id=1, replica_groups=mesh['ctx'=4,'head'=8] {'head'}, use_global_device_ids=true, to_apply=%region_4.5 | all-reduce | flops 2048 | bytes 16384 | tf_op jit(solution)/shard_map/psum | solution.py:173
  120.9 96.0 %reduce-scatter.2.cloned.1.call-done = f32[256,2048]{1,0:T(8,128)} async-done(((f32[2048,2048]{1,0:T(8,128)}), f32[256,2048]{1,0:T(8,128)}) %reduce-scatter.2.cloned.1.call-update) | async-done | bytes 2097168 | tf_op jit(solution)/shard_map/reduce_scatter | solution.py:106
  216.8 2.5 copy.61
  219.3 0.3 fusion.2
  219.7 0.1 convolution_convert_fusion.1
  219.9 0.0 copy-start.5
  219.9 0.5 convolution_convert_fusion
  220.4 1.8 copy.39
  222.2 0.1 copy.42
  222.3 8.1 %all_to_all.10 = bf16[4,2,2,2]{3,1,2,0:T(2,128)(2,1)S(1)} all-to-all(bf16[4,2,2,2]{3,1,2,0:T(2,128)(2,1)S(1)} %copy.42), channel_id=1, replica_groups=mesh['ctx'=4,'head'=8] {'ctx'}, dimensions={0} | all-to-all | bytes 128 | tf_op jit(solution)/shard_map/all_to_all | solution.py:206
  230.4 3.5 %all-to-all-start = ((bf16[4,2,2,128,256]{4,1,3,2,0:T(2,128)(2,1)}), bf16[4,2,2,128,256]{4,1,3,2,0:T(2,128)(2,1)S(1)}, u32[]{:S(2)}, u32[]{:S(2)}) async-start(bf16[4,2,2,128,256]{4,1,3,2,0:T(2,128)(2,1)} %copy.39), calls=%async_computation.1 | async-start | bytes 2097152 | tf_op jit(solution)/shard_map/all_to_all | solution.py:205
  234.0 5.2 %multiply_convert_fusion = bf16[2048,1024]{1,0:T(8,128)(2,1)} fusion(f32[2048,1024]{1,0:T(8,128)} %get-tuple-element.9, f32[1024]{0:T(1024)S(1)} %copy-done.5, f32[2048]{0:T(1024)S(1)} %add_rsqrt_fusion), kind=kLoop, calls=%fused_computation | loop fusion | flops 6291456 | bytes 12595200 | tf_op jit(solution)/shard_map/convert_element_type | solution.py:174
  239.2 0.8 fusion.4
  240.0 4.7 %all-to-all-done = bf16[4,2,2,128,256]{4,1,3,2,0:T(2,128)(2,1)S(1)} async-done(((bf16[4,2,2,128,256]{4,1,3,2,0:T(2,128)(2,1)}), bf16[4,2,2,128,256]{4,1,3,2,0:T(2,128)(2,1)S(1)}, u32[]{:S(2)}, u32[]{:S(2)}) %all-to-all-start) | async-done | bytes 1048608 | tf_op jit(solution)/shard_map/all_to_all | solution.py:205
  244.7 1.6 bitcast_convert_fusion
  246.3 1.2 copy.45
  247.5 0.0 copy-done.1
  (27 shorter events, 0.3 us)
Async XLA Ops:
  8.0 36.9 %copy-start = (s32[32,8,2]{0,2,1:T(2,128)S(1)}, s32[32,8,2]{0,2,1:T(2,128)}, u32[]{:S(2)}) copy-start(s32[32,8,2]{0,2,1:T(2,128)} %param.21) | copy-start | bytes 6148
  8.0 70.9 %all-gather.4.cloned.1.call-start = ((), (), s32[]{:S(2)}) async-start(), calls=%async_computation.4 | async-start | bytes 5242880 | tf_op jit(solution)/shard_map/all_gather | solution.py:142
  10.3 1.2 copy-start.2
  23.2 193.6 %reduce-scatter.2.cloned.1.call-start = ((), (), s32[]{:S(2)}) async-start(), calls=%async_computation.3 | async-start | bytes 18874368 | tf_op jit(solution)/shard_map/reduce_scatter | solution.py:106
  30.1 3.0 %copy-start.7 = (bf16[2048,1024]{1,0:T(8,128)(2,1)S(1)}, bf16[2048,1024]{1,0:T(8,128)(2,1)}, u32[]{:S(2)}) copy-start(bf16[2048,1024]{1,0:T(8,128)(2,1)} %param.11) | copy-start | bytes 12582916
  44.8 0.7 copy-start.8
  44.8 14.7 %copy-start.6 = (f32[16]{0:T(128)S(1)}, f32[16]{0:T(128)}, u32[]{:S(2)}) copy-start(f32[16]{0:T(128)} %param.19) | copy-start | bytes 196
  44.8 36.9 %copy-start.3 = (bf16[2048,256]{1,0:T(8,128)(2,1)S(1)}, bf16[2048,256]{1,0:T(8,128)(2,1)}, u32[]{:S(2)}) copy-start(bf16[2048,256]{1,0:T(8,128)(2,1)} %b_ref.3) | copy-start | bytes 3145732
  81.7 1.2 copy-start.4
  219.9 14.1 %copy-start.5 = (f32[1024]{0:T(1024)S(1)}, f32[1024]{0:T(1024)}, u32[]{:S(2)}) copy-start(f32[1024]{0:T(1024)} %param.20) | copy-start | bytes 12292
  230.4 14.3 %all-to-all-start = ((bf16[4,2,2,128,256]{4,1,3,2,0:T(2,128)(2,1)}), bf16[4,2,2,128,256]{4,1,3,2,0:T(2,128)(2,1)S(1)}, u32[]{:S(2)}, u32[]{:S(2)}) async-start(bf16[4,2,2,128,256]{4,1,3,2,0:T(2,128)(2,1)} %copy.39), calls=%async_computation.1 | async-start | bytes 2097152 | tf_op jit(solution)/shard_map/all_to_all | solution.py:205
  239.2 8.3 %copy-start.1 = (s32[32,8,2]{0,2,1:T(2,128)S(1)}, s32[32,8,2]{0,2,1:T(2,128)}, u32[]{:S(2)}) copy-start(s32[32,8,2]{0,2,1:T(2,128)} %param.21) | copy-start | bytes 6148
Sparse Core Ops, SparseCore 0:
  23.4 55.4 all-gather.3
Sparse Core Ops, SparseCore 1:
  44.9 171.9 reduce-scatter.1

commit v2 on v0

v2 whole, which is shorter than its diff:
```python
import functools
import jax
import jax.numpy as jnp
from jax import lax
from jax.sharding import PartitionSpec as P
from jax.experimental import pallas as pl
from jax.experimental.pallas import tpu as pltpu

NH = 128
P_SIZE = 64
SPAN = 256
HD = 128
PAGE = 256
GROUP = 64


LOG2E = 1.4426950408889634
F32 = jnp.float32


def lanes_of_pair(columns, p, lane_low):
    rows = columns.shape[0]
    first = jnp.broadcast_to(columns[:, 2 * p : 2 * p + 1], (rows, 2 * P_SIZE))
    second = jnp.broadcast_to(columns[:, 2 * p + 1 : 2 * p + 2], (rows, 2 * P_SIZE))
    return jnp.where(lane_low, first, second)


MESH = pl.DeviceIdType.MESH


def block_kernel(
    nw, hc, nctx, attn_h, *refs
):
    w_hs = refs[:nw]
    (x_h, g_h, b_ref, c_ref, col_ref, row_ref, decay_ref, total_ref, skip_ref, gain_ref,
     out_h, kv_ref,
     attn, w_vs, x_v, xs, xr, lr, cs, gated, run, st_own, st, dec, sq,
     load_sem, xs_sem, xr_sem, ls_sem, lr_sem, st_sem, st_rsem, de_sem, de_rsem, sq_sem, sq_rsem,
     out_sem) = refs[nw:]
    q = lax.axis_index("ctx")
    me = lax.axis_index("head")
    zc = hc // 2
    z, core = me // 2, me % 2
    rows, width = x_v.shape
    spans = rows // SPAN
    heads = col_ref.shape[1]

    loads = [pltpu.make_async_copy(attn_h, attn, load_sem.at[0])]
    loads += [pltpu.make_async_copy(w_hs[i], w_vs.at[i], load_sem.at[1 + i]) for i in range(nw)]
    load_x = pltpu.make_async_copy(x_h, x_v, load_sem.at[4])
    load_g = pltpu.make_async_copy(g_h, attn, load_sem.at[5])
    for one in loads:
        one.start()
    load_x.start()

    barrier = pltpu.get_barrier_semaphore()
    for i in range(1, hc):
        pl.semaphore_signal(barrier, inc=1, device_id=(q, lax.rem(me + i, hc)), device_id_type=MESH)
    for i in range(1, nctx):
        pl.semaphore_signal(barrier, inc=1, device_id=(lax.rem(q + i, nctx), me), device_id_type=MESH)
    pl.semaphore_wait(barrier, hc + nctx - 2)
    for one in loads:
        one.wait()

    def tile(k):
        return pl.ds(pl.multiple_of(k * SPAN, SPAN), SPAN)

    def product(dest, dst, kind):
        at = pl.ds(pl.multiple_of(dest * 128, 128), 128)
        w = jnp.concatenate([w_vs[i, :, at] for i in range(nw)], axis=1)

        def step(k, _):
            dst[tile(k), :] = jnp.dot(attn[tile(k), :], w, preferred_element_type=F32).astype(kind)
            return 0

        lax.fori_loop(0, spans, step, 0)

    def pair_copy(t):
        return pltpu.make_async_remote_copy(
            src_ref=xs.at[t], dst_ref=xr.at[t], send_sem=xs_sem.at[t], recv_sem=xr_sem.at[t],
            device_id=(q, 2 * z + 1 - core), device_id_type=MESH)

    def line_copy(t, slot, near):
        return pltpu.make_async_remote_copy(
            src_ref=xs.at[t], dst_ref=lr.at[slot], send_sem=ls_sem.at[t], recv_sem=lr_sem.at[slot],
            device_id=(q, 2 * near + core), device_id_type=MESH)

    def send_up(t):
        line_copy(t, t, z + 1).start()

    def send_down(t):
        line_copy(t, jnp.where(t == z - 1, zc, t), z - 1).start()

    for n in range(zc):
        t = jnp.where(z < zc // 2, zc - 1 - n, n)
        product(2 * t + 1 - core, xs.at[t], jnp.bfloat16)
        pair_copy(t).start()
        product(2 * t + core, cs.at[t], F32)
        pair_copy(t).wait()

        def add(k, _):
            total = cs[t, tile(k), :] + xr[t, tile(k), :].astype(F32)
            cs[t, tile(k), :] = total
            xs[t, tile(k), :] = total.astype(jnp.bfloat16)
            return 0

        lax.fori_loop(0, spans, add, 0)

        @pl.when((z == 0) & (t != z))
        def _():
            send_up(t)

        @pl.when((z == zc - 1) & (t != z))
        def _():
            send_down(t)

    load_g.start()
    load_x.wait()

    def forward(e):
        def pass_on(t):
            line_copy(t, t, z).wait_recv()

            def add(k, _):
                xs[t, tile(k), :] = (cs[t, tile(k), :] + lr[t, tile(k), :].astype(F32)).astype(jnp.bfloat16)
                return 0

            lax.fori_loop(0, spans, add, 0)

        @pl.when((z >= 1) & (z <= e))
        def _():
            t = zc - 1 - e + z
            pass_on(t)
            send_up(t)

        zm = zc - 1 - z

        @pl.when((zm >= 1) & (zm <= e))
        def _():
            t = e - zm
            pass_on(t)
            send_down(t)

    lane_low = lax.broadcasted_iota(jnp.int32, (SPAN, 2 * P_SIZE), 1) < P_SIZE

    def advance(k, p, at, x, weights, b_t):
        decayed = (x * lanes_of_pair(weights, p, lane_low)).astype(jnp.bfloat16)
        part = jnp.dot(b_t, decayed, preferred_element_type=F32)
        run[:, at] = run[:, at] * decay_ref[k, :, at] + part

    run[...] = jnp.zeros_like(run)

    def state_span(k, _):
        cum = col_ref[tile(k), :]
        weights = jnp.exp2(cum[SPAN - 1 :, :] - cum)
        b_t = b_ref[tile(k), :].T
        for p in range(heads // 2):
            at = slice(p * 2 * P_SIZE, (p + 1) * 2 * P_SIZE)
            advance(k, p, at, x_v[tile(k), at].astype(F32), weights, b_t)
        return 0

    lax.fori_loop(0, spans, state_span, 0)
    st_own[...] = run[...].astype(jnp.bfloat16)
    dec[0] = total_ref[...]

    def state_copies(i):
        to = (lax.rem(q + i, nctx), me)
        return (
            pltpu.make_async_remote_copy(
                src_ref=st_own, dst_ref=st.at[i - 1], send_sem=st_sem.at[i - 1],
                recv_sem=st_rsem.at[i - 1], device_id=to, device_id_type=MESH),
            pltpu.make_async_remote_copy(
                src_ref=dec.at[0], dst_ref=dec.at[i], send_sem=de_sem.at[i - 1],
                recv_sem=de_rsem.at[i - 1], device_id=to, device_id_type=MESH),
        )

    for i in range(1, nctx):
        @pl.when(q + i < nctx)
        def _():
            for one in state_copies(i):
                one.start()

    u_at = lax.broadcasted_iota(jnp.int32, (SPAN, SPAN), 1)
    t_at = lax.broadcasted_iota(jnp.int32, (SPAN, SPAN), 0)

    def diag_span(k, _):
        cross = lax.dot_general(
            c_ref[tile(k), :], b_ref[tile(k), :], (((1,), (1,)), ((), ())), preferred_element_type=F32)
        cross = jnp.where(u_at <= t_at, cross, 0.0)
        cum = col_ref[tile(k), :]
        for p in range(heads // 2):
            at = slice(p * 2 * P_SIZE, (p + 1) * 2 * P_SIZE)
            x = x_v[tile(k), at].astype(F32)
            out = skip_ref[:, at] * x
            for i in range(2):
                h = 2 * p + i
                spread = jnp.minimum(cum[:, h : h + 1] - row_ref[h : h + 1, tile(k)], 0.0)
                mixing = (cross * jnp.exp2(spread)).astype(jnp.bfloat16)
                mine = jnp.where(lane_low == (i == 0), x, 0.0).astype(jnp.bfloat16)
                out += jnp.dot(mixing, mine, preferred_element_type=F32)
            gated[tile(k), at] = out
        return 0

    cut = (spans * 3) // 4
    lax.fori_loop(0, cut, diag_span, 0)
    for e in range(1, zc // 2):
        forward(e)
    lax.fori_loop(cut, spans, diag_span, 0)

    run[...] = jnp.zeros_like(run)
    for i in range(nctx - 1, 0, -1):
        @pl.when(q - i >= 0)
        def _():
            for one in state_copies(i):
                one.wait_recv()
            run[...] = run[...] * dec[i, 0:1, :] + st[i - 1].astype(F32)

    load_g.wait()

    def carry_span(k, _):
        cum = col_ref[tile(k), :]
        weights = jnp.exp2(cum[SPAN - 1 :, :] - cum)
        leaving = jnp.exp2(cum)
        b_t = b_ref[tile(k), :].T
        c = c_ref[tile(k), :]
        squares = jnp.zeros((SPAN, 2 * P_SIZE), F32)
        for p in range(heads // 2):
            at = slice(p * 2 * P_SIZE, (p + 1) * 2 * P_SIZE)
            entering = run[:, at].astype(jnp.bfloat16)
            out = gated[tile(k), at] + lanes_of_pair(leaving, p, lane_low) * jnp.dot(
                c, entering, preferred_element_type=F32)
            gate = attn[tile(k), at].astype(F32)
            out = out * (gate / (1.0 + jnp.exp2(gate * -LOG2E)))
            gated[tile(k), at] = out
            squares += out * out
            advance(k, p, at, x_v[tile(k), at].astype(F32), weights, b_t)
        sq[0, :, tile(k)] = jnp.broadcast_to(jnp.sum(squares.T, axis=0, keepdims=True), (8, SPAN))
        return 0

    lax.fori_loop(0, spans, carry_span, 0)

    def square_copy(i):
        return pltpu.make_async_remote_copy(
            src_ref=sq.at[0], dst_ref=sq.at[i], send_sem=sq_sem.at[i - 1], recv_sem=sq_rsem.at[i - 1],
            device_id=(q, lax.rem(me + i, hc)), device_id_type=MESH)

    for i in range(1, hc):
        square_copy(i).start()
    for e in range(zc // 2, zc - 1):
        forward(e)
    for i in range(1, hc):
        square_copy(i).wait_recv()

    def norm_span(k, _):
        total = sq[0, 0:1, tile(k)]
        for i in range(1, hc):
            total += sq[i, 0:1, tile(k)]
        scale = lax.rsqrt(total / (NH * P_SIZE) + 1e-05)
        scale = jnp.broadcast_to(scale, (128, SPAN)).T
        for p in range(width // 128):
            at = slice(p * 128, (p + 1) * 128)
            x_v[tile(k), at] = (gated[tile(k), at] * scale * gain_ref[:, at]).astype(jnp.bfloat16)
        return 0

    lax.fori_loop(0, spans, norm_span, 0)
    store = pltpu.make_async_copy(x_v, out_h, out_sem)
    store.start()

    @pl.when(z > 0)
    def _():
        line_copy(z, z, z).wait_recv()

    @pl.when(z < zc - 1)
    def _():
        line_copy(z, zc, z).wait_recv()

    def last(k, extra):
        total = cs[z, tile(k), :]
        for slot in extra:
            total = total + lr[slot, tile(k), :].astype(F32)
        kv_ref[:, tile(k)] = total.T

    for cond, extra in ((z == 0, (zc,)), (z == zc - 1, (z,)), ((z > 0) & (z < zc - 1), (z, zc))):
        @pl.when(cond)
        def _():
            def step(k, _):
                last(k, extra)
                return 0

            lax.fori_loop(0, spans, step, 0)

    for t in range(zc):
        @pl.when(t != z)
        def _():
            line_copy(t, t, z).wait_send()
    for i in range(1, hc):
        square_copy(i).wait_send()
    for i in range(1, nctx):
        @pl.when(q + i < nctx)
        def _():
            for one in state_copies(i):
                one.wait_send()
    store.wait()


def page_ranks(owner_rows):
    count = owner_rows.shape[-1]
    same = owner_rows[..., :, None] == owner_rows[..., None, :]
    earlier = jnp.arange(count)[None, :] < jnp.arange(count)[:, None]
    return jnp.sum(jnp.logical_and(same, earlier).astype(jnp.int32), axis=-1)


def body(attn_in, w_key, w_value, ssm_in, gate, in_b, in_c, rate, skip, gain, page_table):
    tok_rows, width = ssm_in.shape
    heads_local = rate.shape[0]
    state_dim = in_b.shape[1]
    head_count = lax.axis_size("head")
    ctx_count = lax.axis_size("ctx")
    spans = tok_rows // SPAN
    kv_width = w_key.shape[1] // head_count
    feature_rows = w_key.shape[0]
    if kv_width % 128 == 0:
        weights = (w_key, w_value)
    else:
        shape = (feature_rows, head_count, kv_width)
        weights = (
            jnp.stack((w_key.reshape(shape), w_value.reshape(shape)), axis=2).reshape(
                feature_rows, head_count * 2 * kv_width
            ),
        )
    nw = len(weights)
    chunk = 2 * kv_width
    zc = head_count // 2

    upto = (jnp.arange(SPAN)[:, None] <= jnp.arange(SPAN)[None, :]).astype(F32)
    cum = jnp.einsum(
        "hcu,ut->hct", rate.reshape(heads_local, spans, SPAN) * -LOG2E, upto,
        precision=lax.Precision.HIGHEST,
    )
    span_total = cum[:, :, -1]
    cum_row = cum.reshape(heads_local, tok_rows)
    cum_col = cum_row.T
    decay = jnp.repeat(jnp.exp2(span_total), P_SIZE, axis=0).T.reshape(spans, 1, width)
    total = jnp.repeat(jnp.exp2(jnp.sum(span_total, axis=1)), P_SIZE)
    total = jnp.broadcast_to(total[None, :], (8, width))
    hbm = pl.BlockSpec(memory_space=pl.ANY)
    vmem = pl.BlockSpec(memory_space=pltpu.VMEM)
    bf16 = jnp.bfloat16
    dma = pltpu.SemaphoreType.DMA
    mixer_out, kv_rows = pl.pallas_call(
        functools.partial(block_kernel, nw, head_count, ctx_count),
        in_specs=[hbm] * (nw + 3) + [vmem] * 8,
        out_specs=[hbm, vmem],
        out_shape=[
            jax.ShapeDtypeStruct((tok_rows, width), bf16),
            jax.ShapeDtypeStruct((chunk, tok_rows), F32),
        ],
        scratch_shapes=[
            pltpu.VMEM((tok_rows, width), bf16),
            pltpu.VMEM((nw,) + weights[0].shape, bf16),
            pltpu.VMEM((tok_rows, width), bf16),
            pltpu.VMEM((zc, tok_rows, chunk), bf16),
            pltpu.VMEM((zc, tok_rows, chunk), bf16),
            pltpu.VMEM((zc + 1, tok_rows, chunk), bf16),
            pltpu.VMEM((zc, tok_rows, chunk), F32),
            pltpu.VMEM((tok_rows, width), F32),
            pltpu.VMEM((state_dim, width), F32),
            pltpu.VMEM((state_dim, width), bf16),
            pltpu.VMEM((ctx_count - 1, state_dim, width), bf16),
            pltpu.VMEM((ctx_count, 8, width), F32),
            pltpu.VMEM((head_count, 8, tok_rows), F32),
            dma((6,)),
            dma((zc,)), dma((zc,)), dma((zc,)), dma((zc + 1,)),
            dma((ctx_count - 1,)), dma((ctx_count - 1,)), dma((ctx_count - 1,)), dma((ctx_count - 1,)),
            dma((head_count - 1,)), dma((head_count - 1,)),
            dma,
        ],
        compiler_params=pltpu.CompilerParams(
            vmem_limit_bytes=60 * 1024 * 1024, collective_id=0, has_side_effects=True
        ),
        cost_estimate=pl.CostEstimate(flops=5 * 10**10, bytes_accessed=40 * 2**20, transcendentals=10**7),
    )(attn_in, *weights, ssm_in, gate, in_b, in_c, cum_col, cum_row, decay, total,
      jnp.repeat(skip, P_SIZE).reshape(1, width), gain.reshape(1, width))
    pages_dev = tok_rows // PAGE
    groups = kv_width // GROUP
    by_page = kv_rows.reshape(2, kv_width, pages_dev, PAGE).transpose(2, 0, 1, 3)
    grouped = by_page.reshape(pages_dev, 2, groups, GROUP, PAGE)
    page_max = jnp.max(jnp.abs(grouped), axis=(3, 4))
    quantized = (grouped / (page_max[..., None, None] + 1e-06)).astype(jnp.bfloat16)
    quantized = quantized.reshape(pages_dev, 2, kv_width, PAGE)
    scale_part = page_max.astype(jnp.bfloat16)
    cap_pages = (pages_dev + ctx_count - 1) // ctx_count
    slot_count = min(ctx_count * cap_pages, 2 * pages_dev)
    ctx_index = lax.axis_index("ctx")
    kv_head = lax.axis_index("head") * kv_width // HD
    head_table = lax.dynamic_index_in_dim(page_table, kv_head, 1, keepdims=False)
    owners_all = head_table[:, 0].reshape(ctx_count, pages_dev)
    slots_all = head_table[:, 1].reshape(ctx_count, pages_dev)
    ranks_all = page_ranks(owners_all)
    own_owners = lax.dynamic_index_in_dim(owners_all, ctx_index, 0, keepdims=False)
    own_ranks = lax.dynamic_index_in_dim(ranks_all, ctx_index, 0, keepdims=False)
    owner_hit = jnp.arange(ctx_count)[:, None, None] == own_owners[None, None, :]
    rank_hit = jnp.arange(cap_pages)[None, :, None] == own_ranks[None, None, :]
    send_mask = jnp.logical_and(owner_hit, rank_hit).astype(jnp.bfloat16)
    send_pages = jnp.einsum(
        "oci,iskt->ocskt", send_mask, quantized, preferred_element_type=jnp.float32
    ).astype(jnp.bfloat16)
    send_scales = jnp.einsum(
        "oci,isg->ocsg", send_mask, scale_part, preferred_element_type=jnp.float32
    ).astype(jnp.bfloat16)
    got_pages, got_scales = (
        lax.all_to_all(send_pages, "ctx", split_axis=0, concat_axis=0, tiled=True),
        lax.all_to_all(send_scales, "ctx", split_axis=0, concat_axis=0, tiled=True),
    )
    to_owner = (owners_all == ctx_index)[None, :, None, :]
    rank_match = (ranks_all[:, None, :] == jnp.arange(cap_pages)[None, :, None])[None]
    slot_match = slots_all[None, :, None, :] == jnp.arange(slot_count)[:, None, None, None]
    placement = jnp.sum(
        jnp.logical_and(jnp.logical_and(to_owner, rank_match), slot_match).astype(jnp.float32),
        axis=3,
    ).astype(jnp.bfloat16)
    kv_cache = jnp.einsum(
        "lsc,scakt->lakt", placement, got_pages, preferred_element_type=jnp.float32
    ).astype(jnp.bfloat16)
    kv_scale = jnp.einsum(
        "lsc,scag->lag", placement, got_scales, preferred_element_type=jnp.float32
    ).astype(jnp.bfloat16)
    return (mixer_out, kv_cache, kv_scale)


def solution(mesh):
    in_specs = (
        P("ctx", "head"),
        P("head", None),
        P("head", None),
        P("ctx", "head"),
        P("ctx", "head"),
        P("ctx", None),
        P("ctx", None),
        P("head", "ctx"),
        P("head"),
        P("head"),
        P(),
    )
    out_specs = (P("ctx", "head"), P("ctx", None, "head", None), P("ctx", None, "head"))
    return jax.shard_map(body, mesh=mesh, in_specs=in_specs, out_specs=out_specs, check_vma=False)
```

time: 361 us -> 152 us (0.42)
  local copies, waits for them, and re-layouts: 116 us -> 10.4 us
  Pallas kernels: 0 us -> 102 us
  waiting for transfers between devices: 89 us -> 13.5 us
  other arithmetic: 52.6 us -> 1.94 us
  blocking collectives: 37.8 us -> 0 us
  matrix products: 42.6 us -> 5.14 us
  between operations: 16.5 us -> 0.79 us
  starting transfers between devices: 3.6 us -> 17 us
    pallas_call x0 -> x1, Pallas kernels: none -> 102 us  [body(): pl.pallas_call(functools.partial(block_kernel, nw, head_count, ctx_count)...]
    reduce_scatter x1 -> x0, waiting for transfers between devices: 78.9 us -> none  [body(): lax.psum_scatter(lax.dot_general(w_both, attn_in, (((0,), (1,)), ((), ())...]
    dynamic_slice x16 -> x0, local copies, waits for them, and re-layouts: 44.1 us -> none  [body(): lax.scan(advance, empty_state, (span_total.T, span_state))]
    dot_general x5 -> x1, matrix products: 39.7 us -> 0.24 us  [body(): jnp.einsum('hcu,ut->hct', rate.reshape(heads_local, spans, SPAN) * -LOG2E...]
    unnamed x32 -> x14, local copies, waits for them, and re-layouts: 33.2 us -> 6.56 us
    reshape x4 -> x2, local copies, waits for them, and re-layouts: 22 us -> 0.73 us  [body(): jnp.repeat(jnp.exp2(span_total), P_SIZE, axis=0).T.reshape(spans, 1, width)]
    psum x1 -> x0, blocking collectives: 17.8 us -> none  [body(): square_sum = lax.psum(jnp.sum(gated_out * gated_out, axis=1), 'head')]
    add x8 -> x0, other arithmetic: 16.7 us -> none  [advance(): return (jnp.exp(span_log)[:, None, None] * running + span_sum, running)]
  transfers between devices with their start and end apart: 3 -> 2, of which waited for: 2 -> 2; matrix products, arithmetic and copies ran while one was open for 24% -> 2% of each run, Pallas kernels for 0% -> 0%
where the time goes in v2:
time: 152 us; the launch traced here: 150 us
  Pallas kernels  102 us (67%)
  starting transfers between devices  17 us (11%)
  waiting for transfers between devices  13.5 us (9%)
  local copies, waits for them, and re-layouts  10.4 us (7%)
  matrix products  5.14 us (3%)
  other arithmetic  1.94 us (1%)
    pallas_call x1, Pallas kernels, body(): pl.pallas_call(functools.partial(block_kernel, nw, head_count, ctx_count)...  102 us
    all_to_all x1, starting transfers between devices, body(): lax.all_to_all(send_scales, 'ctx', split_axis=0, concat_axis=0, tiled=True)  13.5 us
    all_to_all x1, waiting for transfers between devices, body(): lax.all_to_all(send_pages, 'ctx', split_axis=0, concat_axis=0, tiled=True)  10.6 us
    unnamed x14, local copies, waits for them, and re-layouts  6.56 us
    all_to_all x1, starting transfers between devices, body(): lax.all_to_all(send_pages, 'ctx', split_axis=0, concat_axis=0, tiled=True)  3.52 us
  transfers between devices with their start and end apart: 2, of which 2 were waited for; matrix products, arithmetic and copies ran while one was open for 2% of the time, Pallas kernels for 0%

profile of v2, /device:TPU:0, one launch (start us, length us, event | category | flops | bytes accessed | tf_op | source)
XLA Modules:
  0.0 150.2 jit_solution(1126281341321905461)
XLA Ops:
  0.6 0.0 copy-start
  0.6 0.0 copy-start.3
  0.7 0.6 copy-done
  1.4 0.1 reshape_squeeze.3
  1.4 0.2 convert_reduce_fusion.1
  1.7 0.9 broadcast_multiply_fusion
  2.7 0.2 fusion.8
  2.9 0.3 slice_reduce_fusion.2
  3.3 0.0 copy-start.2
  3.3 1.3 copy.30.refs_6_
  4.6 0.1 copy.41
  4.7 0.1 broadcast_in_dim.10
  4.8 0.1 reshape.121
  4.9 0.6 reshape.122.refs_8_
  5.5 0.1 broadcast_in_dim.11
  5.6 0.1 broadcast_in_dim.12
  5.7 0.0 copy-done.3
  5.7 0.1 broadcast_in_dim.14
  5.7 0.7 reshape_reshape.3.refs_10_
  6.4 0.6 broadcast_in_dim.13.refs_9_
  7.0 0.0 copy-done.2
  7.0 101.5 %shard_map.130 = (bf16[2048,1024]{1,0:T(8,128)(2,1)}, f32[256,2048]{1,0:T(8,128)}) custom-call(bf16[2048,1024]{1,0:T(8,128)(2,1)} %attn_h.1, bf16[1024,1024]{1,0:T(8,128)(2,1)} %refs_0_.1, bf16[1024,1024]{1,0:T(8,128)(2,1)} %refs_1_.1, bf16[2048,1024]{1,0:T(8,128)(2,1)} %refs_2_.1, bf16[2048,1024]{1,0:T(8,128)(2,1)} %refs_3_.1, bf16[2048,256]{1,0:T(8,128)(2,1)} %refs_4_.1, ...), custom_call_target="tpu_custom_call" | custom-call | flops 49999998976 | bytes 41943040 | tf_op jit(solution)/shard_map/pallas_call | solution.py:350
  108.6 2.5 %copy.45 = f32[32,8,8,256]{3,2,1,0:T(8,128)S(1)} copy(f32[32,8,8,256]{3,1,2,0:T(8,128)} %bitcast.101) | data formatting | bytes 4194304
  111.0 0.3 fusion.2
  111.4 0.8 convolution_convert_fusion.1
  112.2 13.5 %all-to-all-start.1 = ((bf16[4,2,2,2]{3,1,2,0:T(2,128)(2,1)}), bf16[4,2,2,2]{3,1,2,0:T(2,128)(2,1)S(1)}, u32[]{:S(2)}, u32[]{:S(2)}) async-start(bf16[4,2,2,2]{3,1,2,0:T(2,128)(2,1)} %convolution_convert_fusion.1), calls=%async_computation.1 | async-start | bytes 8192 | tf_op jit(solution)/shard_map/all_to_all | solution.py:413
  125.6 1.8 %convolution_convert_fusion = bf16[4,2,2,128,256]{4,1,3,2,0:T(2,128)(2,1)} fusion(f32[8,2,128]{0,2,1:T(8,128)S(1)} %bitcast.108, pred[2,8]{1,0:T(4,128)(4,1)S(1)} %iota_compare_fusion.4, pred[4,8]{1,0:T(4,128)(4,1)S(1)} %iota_compare_fusion.3, f32[2,128,8,256]{3,2,1,0:T(8,128)S(1)} %bitcast.100), kind=kOutput, calls=%fused_computation.6 | convolution fusion | flops 9961536 | bytes 3153968 | tf_op jit(solution)/shard_map/oci,iskt->ocskt/dot_general | solution.py:405
  127.5 2.8 %all-to-all-done.1 = bf16[4,2,2,2]{3,1,2,0:T(2,128)(2,1)S(1)} async-done(((bf16[4,2,2,2]{3,1,2,0:T(2,128)(2,1)}), bf16[4,2,2,2]{3,1,2,0:T(2,128)(2,1)S(1)}, u32[]{:S(2)}, u32[]{:S(2)}) %all-to-all-start.1) | async-done | bytes 96 | tf_op jit(solution)/shard_map/all_to_all | solution.py:413
  130.3 3.5 %all-to-all-start = ((bf16[4,2,2,128,256]{4,1,3,2,0:T(2,128)(2,1)}), bf16[4,2,2,128,256]{4,1,3,2,0:T(2,128)(2,1)S(1)}, u32[]{:S(2)}, u32[]{:S(2)}) async-start(bf16[4,2,2,128,256]{4,1,3,2,0:T(2,128)(2,1)} %convolution_convert_fusion), calls=%async_computation | async-start | bytes 2097152 | tf_op jit(solution)/shard_map/all_to_all | solution.py:412
  133.8 0.1 eq.106
  133.9 0.1 convert_reduce_fusion
  134.0 0.8 fusion.4
  134.8 10.6 %all-to-all-done = bf16[4,2,2,128,256]{4,1,3,2,0:T(2,128)(2,1)S(1)} async-done(((bf16[4,2,2,128,256]{4,1,3,2,0:T(2,128)(2,1)}), bf16[4,2,2,128,256]{4,1,3,2,0:T(2,128)(2,1)S(1)}, u32[]{:S(2)}, u32[]{:S(2)}) %all-to-all-start) | async-done | bytes 1048608 | tf_op jit(solution)/shard_map/all_to_all | solution.py:412
  145.4 0.0 copy-start.1
  145.4 1.6 %bitcast_convert_fusion = bf16[8,2,128,256]{3,0,2,1:T(8,128)(2,1)S(1)} fusion(bf16[4,2,2,128,256]{4,1,3,2,0:T(2,128)(2,1)S(1)} %all-to-all-done, bf16[8,4,2]{0,2,1:T(2,128)(2,1)S(1)} %convert_reduce_fusion), kind=kOutput, calls=%fused_computation.5 | convolution fusion | flops 8912896 | bytes 2097280 | tf_op jit(solution)/shard_map/lsc,scakt->lakt/dot_general | solution.py:422
  147.0 1.2 copy.33
  148.2 0.0 copy-done.1
  148.2 2.0 %copy.47 = bf16[2048,1024]{1,0:T(8,128)(2,1)} copy(bf16[2048,1024]{1,0:T(8,128)(2,1)S(1)} %copy-done.1) | data formatting | bytes 8388608
  (16 shorter events, 0.2 us)
Async XLA Ops:
  0.6 0.7 copy-start
  0.6 5.0 %copy-start.3 = (f32[16]{0:T(128)S(1)}, f32[16]{0:T(128)}, u32[]{:S(2)}) copy-start(f32[16]{0:T(128)} %param.19) | copy-start | bytes 196
  3.3 3.8 %copy-start.2 = (f32[2,8,8,256]{3,1,2,0:T(8,128)}, f32[2,8,8,256]{3,1,2,0:T(8,128)S(1)}, u32[]{:S(2)}) copy-start(f32[2,8,8,256]{3,1,2,0:T(8,128)S(1)} %copy.44) | copy-start | bytes 393220
  112.2 18.1 %all-to-all-start.1 = ((bf16[4,2,2,2]{3,1,2,0:T(2,128)(2,1)}), bf16[4,2,2,2]{3,1,2,0:T(2,128)(2,1)S(1)}, u32[]{:S(2)}, u32[]{:S(2)}) async-start(bf16[4,2,2,2]{3,1,2,0:T(2,128)(2,1)} %convolution_convert_fusion.1), calls=%async_computation.1 | async-start | bytes 8192 | tf_op jit(solution)/shard_map/all_to_all | solution.py:413
  130.3 15.1 %all-to-all-start = ((bf16[4,2,2,128,256]{4,1,3,2,0:T(2,128)(2,1)}), bf16[4,2,2,128,256]{4,1,3,2,0:T(2,128)(2,1)S(1)}, u32[]{:S(2)}, u32[]{:S(2)}) async-start(bf16[4,2,2,128,256]{4,1,3,2,0:T(2,128)(2,1)} %convolution_convert_fusion), calls=%async_computation | async-start | bytes 2097152 | tf_op jit(solution)/shard_map/all_to_all | solution.py:412
  145.4 2.8 %copy-start.1 = (bf16[2048,1024]{1,0:T(8,128)(2,1)S(1)}, bf16[2048,1024]{1,0:T(8,128)(2,1)}, u32[]{:S(2)}) copy-start(bf16[2048,1024]{1,0:T(8,128)(2,1)} %get-tuple-element.28) | copy-start | bytes 12582916

commit v3 on v2

--- a/solution.py
+++ b/solution.py
@@ -32,11 +32,11 @@
     nw, hc, nctx, attn_h, *refs
 ):
     w_hs = refs[:nw]
-    (x_h, g_h, b_ref, c_ref, col_ref, row_ref, decay_ref, total_ref, skip_ref, gain_ref,
-     out_h, kv_ref,
-     attn, w_vs, x_v, xs, xr, lr, cs, gated, run, st_own, st, dec, sq,
+    (x_h, g_h, b_ref, c_ref, col_ref, row_ref, decay_ref, total_ref, skip_ref, gain_ref, idx_ref, sel_ref, pick_ref, valid_ref,
+     out_h, cache_ref, scale_ref,
+     attn, w_vs, x_v, xs, xr, lr, cs, gated, run, st_own, st, dec, sq, pages, going, came, scales,
      load_sem, xs_sem, xr_sem, ls_sem, lr_sem, st_sem, st_rsem, de_sem, de_rsem, sq_sem, sq_rsem,
-     out_sem) = refs[nw:]
+     pg_sem, pg_rsem, sc_sem, sc_rsem, out_sem) = refs[nw:]
     q = lax.axis_index("ctx")
     me = lax.axis_index("head")
     zc = hc // 2
@@ -278,7 +278,14 @@
         total = cs[z, tile(k), :]
         for slot in extra:
             total = total + lr[slot, tile(k), :].astype(F32)
-        kv_ref[:, tile(k)] = total.T
+        by_column = total.T
+        scales[nctx - 1, k] = jnp.zeros((8, 128), F32)
+        for g in range(by_column.shape[0] // GROUP):
+            at = slice(g * GROUP, (g + 1) * GROUP)
+            part = by_column[at, :]
+            most = jnp.max(jnp.max(jnp.abs(part), axis=0, keepdims=True), axis=1, keepdims=True)
+            pages[k, at, :] = (part / (most + 1e-06)).astype(jnp.bfloat16)
+            scales[nctx - 1, k, g : g + 1, :] = jnp.broadcast_to(most, (1, 128))
 
     for cond, extra in ((z == 0, (zc,)), (z == zc - 1, (z,)), ((z > 0) & (z < zc - 1), (z, zc))):
         @pl.when(cond)
@@ -289,6 +296,26 @@
 
             lax.fori_loop(0, spans, step, 0)
 
+    cap = idx_ref.shape[1]
+
+    def page_copies(i):
+        to = (lax.rem(q + i, nctx), me)
+        return (
+            pltpu.make_async_remote_copy(
+                src_ref=going.at[i - 1], dst_ref=came.at[i - 1], send_sem=pg_sem.at[i - 1],
+                recv_sem=pg_rsem.at[i - 1], device_id=to, device_id_type=MESH),
+            pltpu.make_async_remote_copy(
+                src_ref=scales.at[nctx - 1], dst_ref=scales.at[i - 1], send_sem=sc_sem.at[i - 1],
+                recv_sem=sc_rsem.at[i - 1], device_id=to, device_id_type=MESH),
+        )
+
+    for i in range(1, nctx):
+        for n in range(cap):
+            going[i - 1, n] = pages[idx_ref[lax.rem(q + i, nctx), n]]
+        for one in page_copies(i):
+            one.start()
+    for n in range(cap):
+        came[nctx - 1, n] = pages[idx_ref[q, n]]
     for t in range(zc):
         @pl.when(t != z)
         def _():
@@ -300,6 +327,14 @@
         def _():
             for one in state_copies(i):
                 one.wait_send()
+    for i in range(1, nctx):
+        for one in page_copies(i):
+            one.wait()
+    for n in range(cache_ref.shape[0]):
+        keep = valid_ref[n]
+        page = came[sel_ref[n, 0], sel_ref[n, 1]].astype(F32) * keep
+        cache_ref[n] = page.astype(jnp.bfloat16)
+        scale_ref[n] = scales[pick_ref[n, 0], pick_ref[n, 1]] * keep
     store.wait()
 
 
@@ -347,13 +382,44 @@
     vmem = pl.BlockSpec(memory_space=pltpu.VMEM)
     bf16 = jnp.bfloat16
     dma = pltpu.SemaphoreType.DMA
-    mixer_out, kv_rows = pl.pallas_call(
+    pages_dev = tok_rows // PAGE
+    groups = kv_width // GROUP
+    cap_pages = (pages_dev + ctx_count - 1) // ctx_count
+    slot_count = min(ctx_count * cap_pages, 2 * pages_dev)
+    ctx_index = lax.axis_index("ctx")
+    kv_head = lax.axis_index("head") * kv_width // HD
+    head_table = lax.dynamic_index_in_dim(page_table, kv_head, 1, keepdims=False)
+    owners_all = head_table[:, 0].reshape(ctx_count, pages_dev)
+    slots_all = head_table[:, 1].reshape(ctx_count, pages_dev)
+    ranks_all = page_ranks(owners_all)
+    own_owners = lax.dynamic_index_in_dim(owners_all, ctx_index, 0, keepdims=False)
+    own_ranks = lax.dynamic_index_in_dim(ranks_all, ctx_index, 0, keepdims=False)
+    owner_hit = jnp.arange(ctx_count)[:, None, None] == own_owners[None, None, :]
+    rank_hit = jnp.arange(cap_pages)[None, :, None] == own_ranks[None, None, :]
+    page_at = jnp.arange(pages_dev, dtype=jnp.int32)
+    leaving = jnp.sum(jnp.where(owner_hit & rank_hit, page_at[None, None, :], 0), axis=2)
+    apart = (ctx_index - jnp.arange(ctx_count, dtype=jnp.int32)) % ctx_count
+    place = jnp.where(apart == 0, ctx_count - 1, apart - 1)
+    here = (owners_all == ctx_index)[None] & (
+        slots_all[None] == jnp.arange(slot_count)[:, None, None]
+    )
+
+    def chosen(values):
+        values = jnp.broadcast_to(values, owners_all.shape)[None]
+        return jnp.sum(jnp.where(here, values, 0), axis=(1, 2)).astype(jnp.int32)
+
+    select = jnp.stack([chosen(place[:, None]), chosen(ranks_all)], axis=1)
+    pick = jnp.stack([chosen(place[:, None]), chosen(page_at[None, :])], axis=1)
+    filled = jnp.sum(here.astype(F32), axis=(1, 2))
+    smem = pl.BlockSpec(memory_space=pltpu.SMEM)
+    mixer_out, kv_cache, scales = pl.pallas_call(
         functools.partial(block_kernel, nw, head_count, ctx_count),
-        in_specs=[hbm] * (nw + 3) + [vmem] * 8,
-        out_specs=[hbm, vmem],
+        in_specs=[hbm] * (nw + 3) + [vmem] * 8 + [smem] * 4,
+        out_specs=[hbm, vmem, vmem],
         out_shape=[
             jax.ShapeDtypeStruct((tok_rows, width), bf16),
-            jax.ShapeDtypeStruct((chunk, tok_rows), F32),
+            jax.ShapeDtypeStruct((slot_count, chunk, PAGE), bf16),
+            jax.ShapeDtypeStruct((slot_count, 8, 128), F32),
         ],
         scratch_shapes=[
             pltpu.VMEM((tok_rows, width), bf16),
@@ -369,10 +435,15 @@
             pltpu.VMEM((ctx_count - 1, state_dim, width), bf16),
             pltpu.VMEM((ctx_count, 8, width), F32),
             pltpu.VMEM((head_count, 8, tok_rows), F32),
+            pltpu.VMEM((pages_dev, chunk, PAGE), bf16),
+            pltpu.VMEM((ctx_count - 1, cap_pages, chunk, PAGE), bf16),
+            pltpu.VMEM((ctx_count, cap_pages, chunk, PAGE), bf16),
+            pltpu.VMEM((ctx_count, pages_dev, 8, 128), F32),
             dma((6,)),
             dma((zc,)), dma((zc,)), dma((zc,)), dma((zc + 1,)),
             dma((ctx_count - 1,)), dma((ctx_count - 1,)), dma((ctx_count - 1,)), dma((ctx_count - 1,)),
             dma((head_count - 1,)), dma((head_count - 1,)),
+            dma((ctx_count - 1,)), dma((ctx_count - 1,)), dma((ctx_count - 1,)), dma((ctx_count - 1,)),
             dma,
         ],
         compiler_params=pltpu.CompilerParams(
@@ -380,51 +451,10 @@
         ),
         cost_estimate=pl.CostEstimate(flops=5 * 10**10, bytes_accessed=40 * 2**20, transcendentals=10**7),
     )(attn_in, *weights, ssm_in, gate, in_b, in_c, cum_col, cum_row, decay, total,
-      jnp.repeat(skip, P_SIZE).reshape(1, width), gain.reshape(1, width))
-    pages_dev = tok_rows // PAGE
-    groups = kv_width // GROUP
-    by_page = kv_rows.reshape(2, kv_width, pages_dev, PAGE).transpose(2, 0, 1, 3)
-    grouped = by_page.reshape(pages_dev, 2, groups, GROUP, PAGE)
-    page_max = jnp.max(jnp.abs(grouped), axis=(3, 4))
-    quantized = (grouped / (page_max[..., None, None] + 1e-06)).astype(jnp.bfloat16)
-    quantized = quantized.reshape(pages_dev, 2, kv_width, PAGE)
-    scale_part = page_max.astype(jnp.bfloat16)
-    cap_pages = (pages_dev + ctx_count - 1) // ctx_count
-    slot_count = min(ctx_count * cap_pages, 2 * pages_dev)
-    ctx_index = lax.axis_index("ctx")
-    kv_head = lax.axis_index("head") * kv_width // HD
-    head_table = lax.dynamic_index_in_dim(page_table, kv_head, 1, keepdims=False)
-    owners_all = head_table[:, 0].reshape(ctx_count, pages_dev)
-    slots_all = head_table[:, 1].reshape(ctx_count, pages_dev)
-    ranks_all = page_ranks(owners_all)
-    own_owners = lax.dynamic_index_in_dim(owners_all, ctx_index, 0, keepdims=False)
-    own_ranks = lax.dynamic_index_in_dim(ranks_all, ctx_index, 0, keepdims=False)
-    owner_hit = jnp.arange(ctx_count)[:, None, None] == own_owners[None, None, :]
-    rank_hit = jnp.arange(cap_pages)[None, :, None] == own_ranks[None, None, :]
-    send_mask = jnp.logical_and(owner_hit, rank_hit).astype(jnp.bfloat16)
-    send_pages = jnp.einsum(
-        "oci,iskt->ocskt", send_mask, quantized, preferred_element_type=jnp.float32
-    ).astype(jnp.bfloat16)
-    send_scales = jnp.einsum(
-        "oci,isg->ocsg", send_mask, scale_part, preferred_element_type=jnp.float32
-    ).astype(jnp.bfloat16)
-    got_pages, got_scales = (
-        lax.all_to_all(send_pages, "ctx", split_axis=0, concat_axis=0, tiled=True),
-        lax.all_to_all(send_scales, "ctx", split_axis=0, concat_axis=0, tiled=True),
-    )
-    to_owner = (owners_all == ctx_index)[None, :, None, :]
-    rank_match = (ranks_all[:, None, :] == jnp.arange(cap_pages)[None, :, None])[None]
-    slot_match = slots_all[None, :, None, :] == jnp.arange(slot_count)[:, None, None, None]
-    placement = jnp.sum(
-        jnp.logical_and(jnp.logical_and(to_owner, rank_match), slot_match).astype(jnp.float32),
-        axis=3,
-    ).astype(jnp.bfloat16)
-    kv_cache = jnp.einsum(
-        "lsc,scakt->lakt", placement, got_pages, preferred_element_type=jnp.float32
-    ).astype(jnp.bfloat16)
-    kv_scale = jnp.einsum(
-        "lsc,scag->lag", placement, got_scales, preferred_element_type=jnp.float32
-    ).astype(jnp.bfloat16)
+      jnp.repeat(skip, P_SIZE).reshape(1, width), gain.reshape(1, width),
+      leaving.astype(jnp.int32), select, pick, filled)
+    kv_cache = kv_cache.reshape(slot_count, 2, kv_width, PAGE)
+    kv_scale = scales[:, : 2 * groups, 0].astype(bf16).reshape(slot_count, 2, groups)
     return (mixer_out, kv_cache, kv_scale)
 
 

time: 152 us -> 146 us (0.961)
  Pallas kernels: 102 us -> 126 us
  starting transfers between devices: 17 us -> 0 us
  waiting for transfers between devices: 13.5 us -> 0 us
  matrix products: 5.14 us -> 0.23 us
  local copies, waits for them, and re-layouts: 10.4 us -> 14.5 us
    pallas_call x1, Pallas kernels: 102 us -> 126 us  [body(): pl.pallas_call(functools.partial(block_kernel, nw, head_count, ctx_count)...]
    all_to_all x2 -> x0, starting transfers between devices: 17 us -> none  [the longest x1 13.5 us: body(): lax.all_to_all(send_scales, 'ctx', split_axis=0, concat_axis=0, tiled=True)]
    all_to_all x2 -> x0, waiting for transfers between devices: 13.5 us -> none  [the longest x1 10.6 us: body(): lax.all_to_all(send_pages, 'ctx', split_axis=0, concat_axis=0, tiled=True)]
    dot_general x4 -> x0, matrix products: 4.91 us -> none  [the longest x1 1.82 us: body(): jnp.einsum('oci,iskt->ocskt', send_mask, quantized, preferred_element_typ...]
    unnamed x14 -> x11, local copies, waits for them, and re-layouts: 6.56 us -> 6.61 us
  transfers between devices with their start and end apart: 2 -> 0, of which waited for: 2 -> 0; matrix products, arithmetic and copies ran while one was open for 2% -> 0% of each run, Pallas kernels for 0% -> 0%
where the time goes in v3:
time: 146 us; the launch traced here: 144 us
  Pallas kernels  126 us (86%)
  local copies, waits for them, and re-layouts  14.5 us (10%)
  other arithmetic  2.44 us (2%)
    pallas_call x1, Pallas kernels, body(): pl.pallas_call(functools.partial(block_kernel, nw, head_count, ctx_count)...  126 us
    unnamed x11, local copies, waits for them, and re-layouts  6.61 us

profile of v3, /device:TPU:0, one launch (start us, length us, event | category | flops | bytes accessed | tf_op | source)
XLA Modules:
  0.0 143.9 jit_solution(4065871343142855277)
XLA Ops:
  0.6 0.0 copy-start
  0.7 0.7 copy-done
  1.4 0.1 eq.93
  1.5 0.1 reshape_squeeze.3
  1.6 0.6 convert_reduce_fusion.refs_15_
  2.2 0.2 convert_reduce_fusion.1
  2.4 0.2 select_reduce_fusion
  2.6 0.1 select_reduce_fusion.3
  2.8 0.7 copy.34.refs_12_
  3.5 0.7 copy.36.refs_14_
  4.1 0.7 copy.35.refs_13_
  4.8 0.7 broadcast_in_dim.78
  5.5 0.7 reshape_reshape.3.refs_10_
  6.2 0.9 broadcast_multiply_fusion
  7.2 0.2 fusion.1
  7.4 0.3 slice_reduce_fusion.2
  7.7 0.1 copy.38
  7.9 0.1 broadcast_in_dim.75
  7.9 0.1 broadcast_in_dim.76
  8.0 0.6 broadcast_in_dim.77.refs_9_
  8.6 0.1 broadcast_in_dim.74
  8.7 0.1 reshape.107
  8.8 0.6 reshape.108.refs_8_
  9.5 0.0 copy-start.2
  9.5 1.3 copy.33.refs_6_
  10.8 0.0 copy-done.2
  10.8 125.9 %shard_map.130 = (bf16[2048,1024]{1,0:T(8,128)(2,1)}, bf16[8,256,256]{2,1,0:T(8,128)(2,1)}, f32[8,8,128]{2,1,0:T(8,128)}) custom-call(bf16[2048,1024]{1,0:T(8,128)(2,1)} %attn_h.1, bf16[1024,1024]{1,0:T(8,128)(2,1)} %refs_0_.1, bf16[1024,1024]{1,0:T(8,128)(2,1)} %refs_1_.1, bf16[2048,1024]{1,0:T(8,128)(2,1)} %refs_2_.1, bf16[2048,1024]{1,0:T(8,128)(2,1)} %refs_3_.1, ...), custom_call_target="tpu_custom_call" | custom-call | flops 49999998976 | bytes 41943040 | tf_op jit(solution)/shard_map/pallas_call | solution.py:415
  136.7 0.8 slice.23
  137.5 0.7 copy.37
  138.2 0.0 copy-start.1
  138.2 4.7 %copy.44 = bf16[2048,1024]{1,0:T(8,128)(2,1)} copy(bf16[2048,1024]{1,0:T(8,128)(2,1)} %get-tuple-element.23) | data formatting | bytes 8388608
  142.9 0.0 copy-done.1
  142.9 1.0 copy.45
  (13 shorter events, 0.2 us)
Async XLA Ops:
  0.6 0.7 copy-start
  9.5 1.3 copy-start.2
  138.2 4.7 %copy-start.1 = (bf16[8,256,256]{2,1,0:T(8,128)(2,1)S(1)}, bf16[8,256,256]{2,1,0:T(8,128)(2,1)}, u32[]{:S(2)}) copy-start(bf16[8,256,256]{2,1,0:T(8,128)(2,1)} %get-tuple-element.7) | copy-start | bytes 3145732

commit v4 on v3

--- a/solution.py
+++ b/solution.py
@@ -201,7 +201,7 @@
             gated[tile(k), at] = out
         return 0
 
-    cut = (spans * 3) // 4
+    cut = spans // 8
     lax.fori_loop(0, cut, diag_span, 0)
     for e in range(1, zc // 2):
         forward(e)

time: 146 us -> 146 us (level)
  no operation moved by 1% of the time
where the time goes in v4:
time: 146 us; the launch traced here: 144 us
  Pallas kernels  126 us (86%)
  local copies, waits for them, and re-layouts  14.5 us (10%)
  other arithmetic  2.44 us (2%)
    pallas_call x1, Pallas kernels, body(): pl.pallas_call(functools.partial(block_kernel, nw, head_count, ctx_count)...  126 us
    unnamed x11, local copies, waits for them, and re-layouts  6.61 us

profile of v4, /device:TPU:0, one launch (start us, length us, event | category | flops | bytes accessed | tf_op | source)
XLA Modules:
  0.0 143.8 jit_solution(16772010102302851396)
XLA Ops:
  0.6 0.0 copy-start
  0.7 0.7 copy-done
  1.4 0.1 eq.93
  1.5 0.1 reshape_squeeze.3
  1.6 0.6 convert_reduce_fusion.refs_15_
  2.2 0.2 convert_reduce_fusion.1
  2.4 0.2 select_reduce_fusion
  2.6 0.1 select_reduce_fusion.3
  2.8 0.7 copy.34.refs_12_
  3.5 0.7 copy.36.refs_14_
  4.1 0.7 copy.35.refs_13_
  4.8 0.7 broadcast_in_dim.78
  5.5 0.7 reshape_reshape.3.refs_10_
  6.2 0.9 broadcast_multiply_fusion
  7.2 0.2 fusion.1
  7.4 0.3 slice_reduce_fusion.2
  7.7 0.1 copy.38
  7.9 0.1 broadcast_in_dim.75
  7.9 0.1 broadcast_in_dim.76
  8.0 0.6 broadcast_in_dim.77.refs_9_
  8.6 0.1 broadcast_in_dim.74
  8.7 0.1 reshape.107
  8.8 0.6 reshape.108.refs_8_
  9.5 0.0 copy-start.2
  9.5 1.3 copy.33.refs_6_
  10.8 0.0 copy-done.2
  10.8 125.9 %shard_map.130 = (bf16[2048,1024]{1,0:T(8,128)(2,1)}, bf16[8,256,256]{2,1,0:T(8,128)(2,1)}, f32[8,8,128]{2,1,0:T(8,128)}) custom-call(bf16[2048,1024]{1,0:T(8,128)(2,1)} %attn_h.1, bf16[1024,1024]{1,0:T(8,128)(2,1)} %refs_0_.1, bf16[1024,1024]{1,0:T(8,128)(2,1)} %refs_1_.1, bf16[2048,1024]{1,0:T(8,128)(2,1)} %refs_2_.1, bf16[2048,1024]{1,0:T(8,128)(2,1)} %refs_3_.1, ...), custom_call_target="tpu_custom_call" | custom-call | flops 49999998976 | bytes 41943040 | tf_op jit(solution)/shard_map/pallas_call | solution.py:415
  136.7 0.8 slice.23
  137.5 0.7 copy.37
  138.1 0.0 copy-start.1
  138.1 4.7 %copy.44 = bf16[2048,1024]{1,0:T(8,128)(2,1)} copy(bf16[2048,1024]{1,0:T(8,128)(2,1)} %get-tuple-element.23) | data formatting | bytes 8388608
  142.9 0.0 copy-done.1
  142.9 1.0 copy.45
  (13 shorter events, 0.2 us)
Async XLA Ops:
  0.6 0.7 copy-start
  9.5 1.3 copy-start.2
  138.1 4.7 %copy-start.1 = (bf16[8,256,256]{2,1,0:T(8,128)(2,1)S(1)}, bf16[8,256,256]{2,1,0:T(8,128)(2,1)}, u32[]{:S(2)}) copy-start(bf16[8,256,256]{2,1,0:T(8,128)(2,1)} %get-tuple-element.7) | copy-start | bytes 3145732
